TPU v7x, 128 devices: a whole 4x4x4 slice. The times are simulated.
128 devices in a mesh: seq: 32 (over y, z, core), head: 4 (over x).
Axes of the slice: x: 4, y: 4, z: 4, core: 2. Of those that a mesh axis runs over, the one named last changes fastest.
Arguments:
- first_qkv: bfloat16 [3, 2048, 3072], P(None, 'seq', 'head'), may hold values from -64 to 64
- video_qkv: bfloat16 [3, 65536, 3072], P(None, 'seq', 'head'), may hold values from -64 to 64
- head_kind: int32 [24], replicated, may hold values from 0 to 1, as said below
- out_weight: bfloat16 [3072, 3072], P('head', 'seq'), may hold values from -0.109375 to 0.109375
Outputs:
- first_out: bfloat16 [2048, 3072], P('seq', 'head')
- video_out: bfloat16 [65536, 3072], P('seq', 'head')
Inputs may be any that keep to these rules, and one draw needn't show every extreme that they name: `head_kind`: 1 marks a spatial head, 0 a temporal head; each of the 4 aligned groups of 6 consecutive heads holds 2 spatial heads.
All inputs are finite; a program needn't handle non-finite values.
Results may differ from a plain program's by a relative error of at most 0.018.
Values may be sent and summed in bfloat16 or wider, within the bound.
A program may use at most 192 MiB of HBM per device.

v0:
```python
import jax
import jax.numpy as jnp
from jax import lax
from jax.sharding import PartitionSpec as P

HEAD_DIM = 128
SPATIAL = 8
F = 2048


def normalize(scores):
    highest = jnp.max(scores, axis=-1, keepdims=True)
    raised = jnp.exp(scores - highest)
    return (raised / jnp.sum(raised, axis=-1, keepdims=True)).astype(jnp.bfloat16)


def frame_attention(queries, key_rows, value_rows):
    scores = jnp.einsum(
        "qhd,khd->hqk", queries, key_rows, preferred_element_type=jnp.float32
    ) * HEAD_DIM ** (-0.5)
    weights = normalize(scores)
    return jnp.einsum(
        "hqk,khd->qhd", weights, value_rows, preferred_element_type=jnp.float32
    ).astype(jnp.bfloat16)


def per_device(first_qkv, video_qkv, head_kind, out_weight):
    head_count = lax.axis_size("head")
    member = lax.axis_index("head")
    local_heads = first_qkv.shape[-1] // HEAD_DIM
    spatial_count = SPATIAL // head_count
    kinds = head_kind.reshape(head_count, local_heads)
    orders = jnp.argsort(1 - kinds, axis=1, stable=True)
    local_order = lax.dynamic_index_in_dim(orders, member, 0, keepdims=False)
    spatial_heads = local_order[:spatial_count]
    temporal_heads = local_order[spatial_count:]
    first_rows = first_qkv.shape[1]
    frames_here = video_qkv.shape[1] // F
    first = first_qkv.reshape(3, first_rows, local_heads, HEAD_DIM)
    video = video_qkv.reshape(3, frames_here, F, local_heads, HEAD_DIM)
    video_spatial = jnp.moveaxis(jnp.take(video, spatial_heads, axis=3), 1, 0)
    spatial_video = lax.map(
        lambda frame_block: frame_attention(frame_block[0], frame_block[1], frame_block[2]),
        video_spatial,
    )
    first_spatial = jnp.take(first, spatial_heads, axis=2)
    frame_keys, frame_values = (
        lax.all_gather(first_spatial[1], "seq", axis=0, tiled=True),
        lax.all_gather(first_spatial[2], "seq", axis=0, tiled=True),
    )
    spatial_first = frame_attention(first_spatial[0], frame_keys, frame_values)
    sending = jnp.take(video, temporal_heads, axis=3)
    sending = sending.reshape(3, frames_here, F, -1)
    arrived = lax.all_to_all(sending, "seq", split_axis=2, concat_axis=1, tiled=True)
    arrived = arrived.reshape(3, arrived.shape[1], first_rows, -1, HEAD_DIM)
    first_temporal = jnp.take(first, temporal_heads, axis=2)[:, None]
    series = jnp.concatenate([first_temporal, arrived], axis=1)
    scores = jnp.einsum(
        "fphd,gphd->phfg", series[0], series[1], preferred_element_type=jnp.float32
    ) * HEAD_DIM ** (-0.5)
    weights = normalize(scores)
    mixed = jnp.einsum(
        "phfg,gphd->fphd", weights, series[2], preferred_element_type=jnp.float32
    ).astype(jnp.bfloat16)
    temporal_first = mixed[0]
    leaving = mixed[1:].reshape(mixed.shape[0] - 1, first_rows, -1)
    returned = lax.all_to_all(leaving, "seq", split_axis=0, concat_axis=1, tiled=True)
    temporal_video = returned.reshape(frames_here, F, -1, HEAD_DIM)
    video_heads = jnp.concatenate([spatial_video, temporal_video], axis=2).reshape(
        frames_here * F, -1
    )
    first_heads = jnp.concatenate([spatial_first, temporal_first], axis=1).reshape(first_rows, -1)
    attended = jnp.concatenate([first_heads, video_heads], axis=0)
    local_width = attended.shape[1]
    weight_rows = lax.all_gather(out_weight, "seq", axis=1, tiled=True)
    weight_blocks = lax.all_to_all(weight_rows, "head", split_axis=1, concat_axis=0, tiled=True)
    weight_blocks = weight_blocks.reshape(head_count, local_heads, HEAD_DIM, -1)
    all_heads = lax.all_gather(attended, "head", axis=1, tiled=True)
    summed = jnp.zeros((attended.shape[0], weight_blocks.shape[-1]), jnp.float32)
    for holder in range(head_count):
        reordered = jnp.take(weight_blocks[holder], orders[holder], axis=0).reshape(local_width, -1)
        columns = all_heads[:, holder * local_width : (holder + 1) * local_width]
        partial_value = jnp.dot(columns, reordered, preferred_element_type=jnp.float32).astype(
            jnp.bfloat16
        )
        partial_value = lax.optimization_barrier(partial_value)
        summed = summed + partial_value.astype(jnp.float32)
    result = summed.astype(jnp.bfloat16)
    return (result[:first_rows], result[first_rows:])


def solution(mesh):
    in_specs = (P(None, "seq", "head"), P(None, "seq", "head"), P(), P("head", "seq"))
    out_specs = (P("seq", "head"), P("seq", "head"))
    return jax.shard_map(
        per_device, mesh=mesh, in_specs=in_specs, out_specs=out_specs, check_vma=False
    )
```

profile of v0, /device:TPU:2, one launch (start us, length us, event | category | flops | bytes accessed | tf_op | source)
XLA Modules:
  0.0 481.9 jit_solution(11714190869684210275)
XLA Ops:
  7.2 0.7 broadcast_subtract_fusion
  8.1 0.7 sort.17
  9.2 0.6 gather_fusion
  9.9 0.6 fusion.50
  10.7 12.7 %copy.61 = bf16[3,2048,768]{1,2,0:T(8,128)(2,1)} copy(bf16[3,2048,768]{2,1,0:T(8,128)(2,1)} %param.7) | data formatting | bytes 18874368 | tf_op args[1]
  23.4 9.2 %copy.62 = bf16[3,2048,6,128]{1,3,0,2:T(8,128)(2,1)} copy(bf16[3,2048,6,128]{1,3,2,0:T(8,128)(2,1)} %bitcast.104) | data formatting | bytes 18874368 | tf_op jit(solution)/shard_map/reshape | solution.py:40
  32.6 7.3 %gather_fusion.2 = bf16[4,3,2048,128]{2,3,1,0:T(8,128)(2,1)} fusion(bf16[3,2048,6,128]{1,3,0,2:T(8,128)(2,1)} %copy.62, s32[1024]{0:T(1024)S(1)} %pad_clamp_fusion.4), kind=kCustom, calls=%fused_computation.6 | custom fusion | bytes 12582928 | tf_op jit(solution)/shard_map/jit(_take)/gather | solution.py:52
  39.9 3.4 copy.63
  43.4 3.7 bitcast_select_fusion
  47.1 14.1 %copy.64 = bf16[3,1,2048,512]{3,0,1,2:T(4,128)(2,1)} copy(bf16[3,1,2048,512]{2,3,0,1:T(8,128)(2,1)} %bitcast_select_fusion) | data formatting | bytes 12582912 | tf_op jit(solution)/shard_map/jit(_take)/select_n | solution.py:52
  61.2 8.5 %all-to-all-start = ((bf16[3,1,2048,512]{3,0,1,2:T(4,128)(2,1)}), bf16[3,1,2048,512]{3,0,1,2:T(4,128)(2,1)}, u32[]{:S(2)}, u32[]{:S(2)}) async-start(bf16[3,1,2048,512]{3,0,1,2:T(4,128)(2,1)} %copy.64), calls=%async_computation | async-start | bytes 16777216 | tf_op jit(solution)/shard_map/all_to_all | solution.py:54
  69.8 0.7 all-gather.11.cloned.1.call-update
  70.5 0.5 all-gather.9.cloned.1.call-start
  71.2 0.6 gather_fusion.1
  71.8 6.1 %gather_fusion.3 = bf16[2,3,2048,128]{2,3,1,0:T(8,128)(2,1)} fusion(bf16[3,2048,6,128]{1,3,0,2:T(8,128)(2,1)} %copy.62, s32[1024]{0:T(1024)S(1)} %pad_clamp_fusion.5), kind=kCustom, calls=%fused_computation.7 | custom fusion | bytes 6291464 | tf_op jit(solution)/shard_map/jit(_take)/gather | solution.py:41
  77.9 3.5 copy.71
  81.4 1.2 broadcast_select_fusion.4
  82.6 2.0 bitcast_select_fusion.1
  84.6 18.2 %fusion.52 = (f32[2,2048]{1,0:T(2,128)S(1)}, f32[2,2048,2048]{1,2,0:T(8,128)}) fusion(bf16[3,1,2048,2,128]{4,2,3,1,0:T(8,128)(2,1)} %bitcast_select_fusion.1), kind=kOutput, calls=%fused_computation.116 | convolution fusion | flops 2172651520 | bytes 35667968 | tf_op jit(solution)/shard_map/while/body/eval_jaxpr/sub | solution.py:13
  102.9 81.4 %all-to-all-done = bf16[3,1,2048,512]{3,0,1,2:T(4,128)(2,1)} async-done(((bf16[3,1,2048,512]{3,0,1,2:T(4,128)(2,1)}), bf16[3,1,2048,512]{3,0,1,2:T(4,128)(2,1)}, u32[]{:S(2)}, u32[]{:S(2)}) %all-to-all-start) | async-done | bytes 6291488 | tf_op jit(solution)/shard_map/all_to_all | solution.py:54
  184.3 17.7 %reshape.274 = bf16[3,32,64,4,128]{4,3,0,2,1:T(4,128)(2,1)} reshape(bf16[3,1,2048,512]{3,0,1,2:T(4,128)(2,1)} %all-to-all-done) | data formatting | bytes 12582912 | tf_op jit(solution)/shard_map/reshape | solution.py:55
  201.9 10.2 %copy.66 = bf16[3,32,64,4,128]{4,1,3,2,0:T(8,128)(2,1)S(1)} copy(bf16[3,32,64,4,128]{4,3,0,2,1:T(4,128)(2,1)} %reshape.274) | data formatting | bytes 12582912 | tf_op jit(solution)/shard_map/reshape | solution.py:55
  212.1 1.9 fusion.20
  214.0 10.6 %fusion.51 = (f32[64,4,33]{2,1,0:T(4,128)S(1)}, f32[64,4,33,33]{2,3,1,0:T(8,128)S(1)}) fusion(f32[64,4,33,33]{2,3,1,0:T(8,128)S(1)} %fusion.20), kind=kOutput, calls=%fused_computation.115 | output fusion | flops 1115168 | bytes 2264064 | tf_op jit(solution)/shard_map/sub | solution.py:13
  224.6 1.9 convert_bitcast_fusion
  226.5 1.4 copy-done.5
  227.9 1.2 slice.159
  229.1 1.1 copy.74
  230.2 2.4 reshape.182
  232.6 20.2 %all-to-all-start.1 = ((bf16[32,64,512]{2,1,0:T(8,128)(2,1)}), bf16[32,64,512]{2,1,0:T(8,128)(2,1)S(1)}, u32[]{:S(2)}, u32[]{:S(2)}) async-start(bf16[32,64,512]{2,1,0:T(8,128)(2,1)} %reshape.182), calls=%async_computation.1 | async-start | bytes 4194304 | tf_op jit(solution)/shard_map/all_to_all | solution.py:67
  252.8 13.3 %fusion.33 = bf16[1,2048,2,128]{1,3,2,0:T(8,128)(2,1)} fusion(f32[2,2048,2048]{1,2,0:T(8,128)} %get-tuple-element.28, f32[2,2048]{1,0:T(2,128)S(1)} %get-tuple-element.27, bf16[3,1,2048,2,128]{4,2,3,1,0:T(8,128)(2,1)} %bitcast_select_fusion.1), kind=kOutput, calls=%fused_computation.55 | convolution fusion | flops 2164785152 | bytes 35667968 | tf_op jit(solution)/shard_map/while/body/eval_jaxpr/hqk,khd->qhd/dot_general | solution.py:22
  266.1 1.7 convolution_multiply_fusion
  267.8 0.3 fusion.53
  268.1 1.7 fusion.36
  269.8 1.1 slice.155
  271.2 10.5 %all-to-all-done.1 = bf16[32,64,512]{2,1,0:T(8,128)(2,1)S(1)} async-done(((bf16[32,64,512]{2,1,0:T(8,128)(2,1)}), bf16[32,64,512]{2,1,0:T(8,128)(2,1)S(1)}, u32[]{:S(2)}, u32[]{:S(2)}) %all-to-all-start.1) | async-done | bytes 2097184 | tf_op jit(solution)/shard_map/all_to_all | solution.py:67
  281.7 2.0 reshape.183
  283.7 3.0 copy.75
  286.7 0.3 pad_maximum_fusion.1
  287.0 3.5 pad_maximum_fusion
  290.6 5.5 %all-to-all-start.2 = ((bf16[768,4,768]{0,2,1:T(8,128)(2,1)}), bf16[768,4,768]{0,2,1:T(8,128)(2,1)}, u32[]{:S(2)}, u32[]{:S(2)}) async-start(bf16[768,4,768]{0,2,1:T(8,128)(2,1)} %bitcast.111), calls=%async_computation.2 | async-start | bytes 9437184 | tf_op jit(solution)/shard_map/all_to_all | solution.py:76
  296.1 97.4 %all-to-all-done.2 = bf16[768,4,768]{0,2,1:T(8,128)(2,1)} async-done(((bf16[768,4,768]{0,2,1:T(8,128)(2,1)}), bf16[768,4,768]{0,2,1:T(8,128)(2,1)}, u32[]{:S(2)}, u32[]{:S(2)}) %all-to-all-start.2) | async-done | bytes 4718624 | tf_op jit(solution)/shard_map/all_to_all | solution.py:76
  393.5 4.2 fusion.49
  397.7 2.4 copy.77
  400.1 2.4 copy.78
  402.5 1.4 copy.79
  403.9 1.7 copy.80
  405.6 3.1 gather_fusion.4
  408.7 1.9 gather_fusion.5
  410.6 1.7 gather_fusion.6
  412.3 1.9 gather_fusion.7
  414.2 2.6 broadcast_select_fusion.3
  416.8 1.2 broadcast_select_fusion.2
  418.0 1.2 broadcast_select_fusion.1
  419.2 1.2 broadcast_select_fusion
  420.4 35.9 %all-gather.7.cloned.1.call-done = bf16[2112,3072]{0,1:T(8,128)(2,1)} async-done(((bf16[2112,768]{0,1:T(8,128)(2,1)}), bf16[2112,3072]{0,1:T(8,128)(2,1)}) %all-gather.7.cloned.1.call-update) | async-done | bytes 12976144 | tf_op jit(solution)/shard_map/all_gather | solution.py:78
  456.3 4.8 %convolution_convert_fusion.3 = bf16[2112,768]{1,0:T(8,128)(2,1)S(1)} fusion(bf16[768,768]{1,0:T(8,128)(2,1)S(1)} %bitcast.112, bf16[2112,3072]{0,1:T(8,128)(2,1)} %all-gather.7.cloned.1.call-done), kind=kOutput, calls=%fused_computation.28 | convolution fusion | flops 2493038592 | bytes 7766016 | tf_op jit(solution)/shard_map/dot_general | solution.py:83
  461.1 1.3 copy-done.11
  462.5 2.7 convolution_convert_fusion.2
  465.2 2.7 convolution_convert_fusion.1
  468.0 2.7 convolution_convert_fusion
  470.7 1.7 add_convert_fusion
  472.4 1.9 slice.169
  474.2 0.6 slice.168
  (57 shorter events, 1.6 us)
Async XLA Ops:
  7.2 2.0 copy-start
  7.2 258.9 %all-gather.13.cloned.1.call-start = ((), (), s32[]{:S(2)}) async-start(), calls=%async_computation.6 | async-start | bytes 1081344 | tf_op jit(solution)/shard_map/all_gather | solution.py:48
  61.2 123.0 %all-to-all-start = ((bf16[3,1,2048,512]{3,0,1,2:T(4,128)(2,1)}), bf16[3,1,2048,512]{3,0,1,2:T(4,128)(2,1)}, u32[]{:S(2)}, u32[]{:S(2)}) async-start(bf16[3,1,2048,512]{3,0,1,2:T(4,128)(2,1)} %copy.64), calls=%async_computation | async-start | bytes 16777216 | tf_op jit(solution)/shard_map/all_to_all | solution.py:54
  69.8 198.4 %all-gather.11.cloned.1.call-start = ((), (), s32[]{:S(2)}) async-start(), calls=%async_computation.5 | async-start | bytes 1081344 | tf_op jit(solution)/shard_map/all_gather | solution.py:49
  70.5 220.0 %all-gather.9.cloned.1.call-start = ((), (), s32[]{:S(2)}) async-start(), calls=%async_computation.4 | async-start | bytes 4866048 | tf_op jit(solution)/shard_map/all_gather | solution.py:75
  201.9 10.2 %copy-start.4 = (bf16[3,1,64,4,128]{4,1,3,2,0:T(2,128)(2,1)S(1)}, bf16[3,1,64,4,128]{4,1,3,2,0:T(2,128)(2,1)}, u32[]{:S(2)}) copy-start(bf16[3,1,64,4,128]{4,1,3,2,0:T(2,128)(2,1)} %broadcast_select_fusion.4) | copy-start | bytes 589828
  226.4 1.4 copy-start.5
  232.6 49.1 %all-to-all-start.1 = ((bf16[32,64,512]{2,1,0:T(8,128)(2,1)}), bf16[32,64,512]{2,1,0:T(8,128)(2,1)S(1)}, u32[]{:S(2)}, u32[]{:S(2)}) async-start(bf16[32,64,512]{2,1,0:T(8,128)(2,1)} %reshape.182), calls=%async_computation.1 | async-start | bytes 4194304 | tf_op jit(solution)/shard_map/all_to_all | solution.py:67
  252.8 203.5 %all-gather.7.cloned.1.call-start = ((), (), s32[]{:S(2)}) async-start(), calls=%async_computation.3 | async-start | bytes 16711680 | tf_op jit(solution)/shard_map/all_gather | solution.py:78
  271.2 15.5 %copy-start.10 = (bf16[1,2048,2,128]{1,3,2,0:T(8,128)(2,1)S(1)}, bf16[1,2048,2,128]{1,3,2,0:T(8,128)(2,1)}, u32[]{:S(2)}) copy-start(bf16[1,2048,2,128]{1,3,2,0:T(8,128)(2,1)} %fusion.33) | copy-start | bytes 3145732
  290.6 103.0 %all-to-all-start.2 = ((bf16[768,4,768]{0,2,1:T(8,128)(2,1)}), bf16[768,4,768]{0,2,1:T(8,128)(2,1)}, u32[]{:S(2)}, u32[]{:S(2)}) async-start(bf16[768,4,768]{0,2,1:T(8,128)(2,1)} %bitcast.111), calls=%async_computation.2 | async-start | bytes 9437184 | tf_op jit(solution)/shard_map/all_to_all | solution.py:76
  405.6 5.0 %copy-start.3 = (bf16[1,768,768]{2,1,0:T(8,128)(2,1)S(1)}, bf16[1,768,768]{2,1,0:T(8,128)(2,1)}, u32[]{:S(2)}) copy-start(bf16[1,768,768]{2,1,0:T(8,128)(2,1)} %copy.79) | copy-start | bytes 3538948
  414.2 3.8 copy-start.2
  418.0 38.3 %copy-start.6 = (bf16[6,128,768]{2,1,0:T(8,128)(2,1)S(1)}, bf16[6,128,768]{2,1,0:T(8,128)(2,1)}, u32[]{:S(2)}) copy-start(bf16[6,128,768]{2,1,0:T(8,128)(2,1)} %broadcast_select_fusion.3) | copy-start | bytes 3538948
  456.3 4.8 %copy-start.7 = (bf16[6,128,768]{2,1,0:T(8,128)(2,1)S(1)}, bf16[6,128,768]{2,1,0:T(8,128)(2,1)}, u32[]{:S(2)}) copy-start(bf16[6,128,768]{2,1,0:T(8,128)(2,1)} %broadcast_select_fusion.2) | copy-start | bytes 3538948
  456.3 6.2 %copy-start.11 = (bf16[2112,3072]{0,1:T(8,128)(2,1)S(1)}, bf16[2112,3072]{0,1:T(8,128)(2,1)}, u32[]{:S(2)}) copy-start(bf16[2112,3072]{0,1:T(8,128)(2,1)} %all-gather.7.cloned.1.call-done) | copy-start | bytes 38928388
  462.5 2.7 copy-start.8
  465.2 2.7 copy-start.9
  470.7 4.2 copy-start.1
Sparse Core Ops, SparseCore 0:
  11.0 45.3 all-gather.12
  73.0 106.2 all-gather.10
  181.5 47.9 all-gather.8
  290.6 165.5 all-gather.6
where the time goes:
time: 490 us; the launch traced here: 482 us
  waiting for transfers between devices  226 us (46%)
  local copies, waits for them, and re-layouts  124 us (25%)
  matrix products  51.7 us (11%)
  starting transfers between devices  34.7 us (7%)
  other arithmetic  31 us (6%)
  between operations  14.6 us (3%)
    all_to_all x1, waiting for transfers between devices, per_device(): lax.all_to_all(weight_rows, 'head', split_axis=1, concat_axis=0, tiled=True)  97.4 us
    all_to_all x1, waiting for transfers between devices, per_device(): lax.all_to_all(sending, 'seq', split_axis=2, concat_axis=1, tiled=True)  81.4 us
    all_gather x1, waiting for transfers between devices, per_device(): all_heads = lax.all_gather(attended, 'head', axis=1, tiled=True)  35.9 us
    reshape x2, local copies, waits for them, and re-layouts, per_device(): arrived = arrived.reshape(3, arrived.shape[1], first_rows, -1, HEAD_DIM)  27.8 us
    all_to_all x1, starting transfers between devices, per_device(): lax.all_to_all(leaving, 'seq', split_axis=0, concat_axis=1, tiled=True)  20.2 us
    sub x1, matrix products, normalize(): raised = jnp.exp(scores - highest)  18.2 us
    unnamed x25, local copies, waits for them, and re-layouts  15.5 us
    dot_general x2, matrix products, frame_attention(): jnp.einsum('hqk,khd->qhd', weights, value_rows, preferred_element_type=jn...  14.9 us
  transfers between devices with their start and end apart: 7, of which 4 were waited for; matrix products, arithmetic and copies ran while one was open for 38% of the time, Pallas kernels for 0%

commit v1 on v0

v1 whole, which is shorter than its diff:
```python
import functools

import jax
import jax.numpy as jnp
from jax import lax
from jax.experimental import pallas as pl
from jax.experimental.pallas import tpu as pltpu
from jax.sharding import PartitionSpec as P

HEAD_DIM = 128
F = 2048
SEQ = 32
LOCAL = 6
NS = 2
NT = 4
CHUNKS = 4
TILE = 16
WIDTH = LOCAL * HEAD_DIM
SW = NS * HEAD_DIM
TW = NT * HEAD_DIM
FRAMES = SEQ + 1
ROWS = FRAMES * TILE
EXP_SCALE = HEAD_DIM ** (-0.5) * 1.4426950408889634
MASKED = -1e30
MESH = pl.DeviceIdType.MESH
NT_DIMS = (((1,), (1,)), ((), ()))


def kernel(
    kinds, first_hbm, video_hbm, kv_hbm, w_hbm, first_out, video_out,
    first, stage, spatial, kv, weight, send, recv, back, act, part_send, part_recv, out_buf, bias,
    load_sem, const_sem, send_sem, recv_sem, back_send_sem, back_recv_sem,
    sp_send_sem, sp_recv_sem, ag_send_sem, ag_recv_sem, rs_send_sem, rs_recv_sem, out_sem,
):
    s = lax.axis_index("seq")
    g = lax.axis_index("head")
    near = jnp.bitwise_xor(g, 1)
    far = 3 - g

    def load(c):
        return pltpu.make_async_copy(
            video_hbm.at[:, :, pl.ds(c * TILE, TILE)], stage.at[c % 2], load_sem.at[c % 2]
        )

    load(0).start()
    load(1).start()
    first_copy = pltpu.make_async_copy(first_hbm, first, const_sem.at[0])
    first_copy.start()
    kv_copy = pltpu.make_async_copy(kv_hbm, kv, const_sem.at[1])
    kv_copy.start()
    w_copy = pltpu.make_async_copy(w_hbm, weight, const_sem.at[2])
    w_copy.start()

    barrier = pltpu.get_barrier_semaphore()

    def greet(k, carry):
        pl.semaphore_signal(
            barrier, inc=1, device_id=(jnp.bitwise_xor(s, k), g), device_id_type=MESH
        )
        return carry

    lax.fori_loop(1, SEQ, greet, 0)
    for other in (near, far):
        pl.semaphore_signal(barrier, inc=1, device_id=(s, other), device_id_type=MESH)

    kind = [kinds[g * LOCAL + h] for h in range(LOCAL)]
    takes = []
    for slot in range(LOCAL):
        want, rank = (1, slot) if slot < NS else (0, slot - NS)
        seen = jnp.int32(0)
        row = []
        for h in range(LOCAL):
            is_kind = kind[h] == want
            row.append(jnp.logical_and(is_kind, seen == rank))
            seen = seen + jnp.where(is_kind, 1, 0)
        takes.append(row)

    def pick(slot, heads):
        low, count = (slot, 5) if slot < NS else (slot - NS, 3)
        value = heads[low]
        for h in range(low + 1, low + count):
            value = lax.select(takes[slot][h], heads[h], value)
        return value

    def split(tile):
        return [tile[:, h * HEAD_DIM : (h + 1) * HEAD_DIM] for h in range(LOCAL)]

    row_id = lax.broadcasted_iota(jnp.int32, (TILE, ROWS), 0)
    col_id = lax.broadcasted_iota(jnp.int32, (TILE, ROWS), 1)
    bias[...] = jnp.where(row_id == jnp.bitwise_and(col_id, TILE - 1), 0.0, MASKED)

    first_copy.wait()
    for c in range(CHUNKS):
        for plane in range(3):
            heads = split(first[plane, c * TILE : (c + 1) * TILE, :])
            for slot in range(NT):
                recv[c, 0, plane, :, slot * HEAD_DIM : (slot + 1) * HEAD_DIM] = pick(
                    NS + slot, heads
                )
            if plane == 0:
                for slot in range(NS):
                    act[c, 0, :, slot * HEAD_DIM : (slot + 1) * HEAD_DIM] = pick(slot, heads)

    pl.semaphore_wait(barrier, SEQ + 1)

    for c in range(CHUNKS):
        load(c).wait()

        def pack(d, carry):
            for plane in range(3):
                heads = split(stage[c % 2, plane, d])
                for slot in range(NT):
                    send[c, d, plane, :, slot * HEAD_DIM : (slot + 1) * HEAD_DIM] = pick(
                        NS + slot, heads
                    )
                start = pl.multiple_of(d * (CHUNKS * TILE) + c * TILE, TILE)
                for slot in range(NS):
                    spatial[plane, slot, pl.ds(start, TILE), :] = pick(slot, heads)
            return carry

        lax.fori_loop(0, SEQ, pack, 0)
        if c + 2 < CHUNKS:
            load(c + 2).start()

        def post(k, carry):
            d = jnp.bitwise_xor(s, k)
            pltpu.make_async_remote_copy(
                src_ref=send.at[c, d], dst_ref=recv.at[c, 1 + s],
                send_sem=send_sem.at[c], recv_sem=recv_sem.at[c],
                device_id=(d, g), device_id_type=MESH,
            ).start()
            return carry

        lax.fori_loop(1, SEQ, post, 0)
        pltpu.make_async_copy(send.at[c, s], recv.at[c, 1 + s], recv_sem.at[c]).start()

    def attend(q, k, v, mask):
        scores = lax.dot_general(q, k, NT_DIMS, preferred_element_type=jnp.float32)
        if mask is not None:
            scores = (scores.reshape(FRAMES, TILE, ROWS) + mask[None]).reshape(ROWS, ROWS)
        top = jnp.max(scores, axis=-1, keepdims=True)
        raised = jnp.exp2((scores - top) * EXP_SCALE)
        total = jnp.sum(raised, axis=-1, keepdims=True)
        mixed = jnp.dot(raised.astype(jnp.bfloat16), v, preferred_element_type=jnp.float32)
        return (mixed / total).astype(jnp.bfloat16)

    block = 256
    for h in range(NS):
        columns = slice(h * HEAD_DIM, (h + 1) * HEAD_DIM)

        def frame_block(b, carry):
            start = pl.multiple_of(b * block, block)
            mixed = attend(spatial[0, h, pl.ds(start, block), :], spatial[1, h], spatial[2, h], None)
            for dd in range(block // (CHUNKS * TILE)):
                for c in range(CHUNKS):
                    at = (dd * CHUNKS + c) * TILE
                    act[c, 1 + b * (block // (CHUNKS * TILE)) + dd, :, columns] = mixed[at : at + TILE]
            return carry

        lax.fori_loop(0, F // block, frame_block, 0)

    kv_copy.wait()
    for h in range(NS):
        columns = slice(h * HEAD_DIM, (h + 1) * HEAD_DIM)
        queries = act[:, 0, :, columns].reshape(CHUNKS * TILE, HEAD_DIM)
        mixed = attend(queries, kv[0, :, columns], kv[1, :, columns], None)
        for c in range(CHUNKS):
            act[c, 0, :, columns] = mixed[c * TILE : (c + 1) * TILE]

    sp_copy = pltpu.make_async_remote_copy(
        src_ref=act.at[:, :, :, pl.ds(0, SW)], dst_ref=act.at[:, :, :, pl.ds(WIDTH, SW)],
        send_sem=sp_send_sem, recv_sem=sp_recv_sem,
        device_id=(s, near), device_id_type=MESH,
    )
    sp_copy.start()

    def temporal(c):
        pltpu.make_async_copy(
            recv.at[c, pl.ds(1, SEQ)], recv.at[c, pl.ds(1, SEQ)], recv_sem.at[c]
        ).wait()

        def one_head(t, carry):
            columns = pl.ds(pl.multiple_of(t * HEAD_DIM, HEAD_DIM), HEAD_DIM)
            q, k, v = (
                recv[c, :, plane, :, columns].reshape(ROWS, HEAD_DIM) for plane in range(3)
            )
            mixed = attend(q, k, v, bias[...])
            back[c, :, :, columns] = mixed.reshape(FRAMES, TILE, HEAD_DIM)
            return carry

        lax.fori_loop(0, NT, one_head, 0)

        def post(k, carry):
            d = jnp.bitwise_xor(s, k)
            pltpu.make_async_remote_copy(
                src_ref=back.at[c, 1 + d], dst_ref=act.at[c, 1 + s, :, pl.ds(SW, TW)],
                send_sem=back_send_sem.at[c], recv_sem=back_recv_sem.at[c],
                device_id=(d, g), device_id_type=MESH,
            ).start()
            return carry

        lax.fori_loop(1, SEQ, post, 0)
        pltpu.make_async_copy(
            back.at[c, 1 + s], act.at[c, 1 + s, :, pl.ds(SW, TW)], back_recv_sem.at[c]
        ).start()
        act[c, 0, :, SW:WIDTH] = back[c, 0]

    def ag_copy(c):
        return pltpu.make_async_remote_copy(
            src_ref=act.at[c, :, :, pl.ds(SW, TW)], dst_ref=act.at[c, :, :, pl.ds(WIDTH + SW, TW)],
            send_sem=ag_send_sem.at[c], recv_sem=ag_recv_sem.at[c],
            device_id=(s, near), device_id_type=MESH,
        )

    def share(c):
        landed = act.at[c, pl.ds(1, SEQ), :, pl.ds(SW, TW)]
        pltpu.make_async_copy(landed, landed, back_recv_sem.at[c]).wait()
        ag_copy(c).start()

    def rs_copy(c):
        return pltpu.make_async_remote_copy(
            src_ref=part_send.at[c], dst_ref=part_recv.at[c],
            send_sem=rs_send_sem.at[c], recv_sem=rs_recv_sem.at[c],
            device_id=(s, far), device_id_type=MESH,
        )

    def project(c, which):
        return lax.dot_general(
            act[c].reshape(ROWS, 2 * WIDTH), weight[which], NT_DIMS,
            preferred_element_type=jnp.float32,
        )

    def partial(c):
        if c == 0:
            sp_copy.wait_recv()
            w_copy.wait()
        ag_copy(c).wait_recv()
        part_send[c] = project(c, 1).astype(jnp.bfloat16).reshape(FRAMES, TILE, WIDTH)
        rs_copy(c).start()

    def out_copies(c):
        return (
            pltpu.make_async_copy(
                out_buf.at[c % 2, pl.ds(1, SEQ)], video_out.at[:, pl.ds(c * TILE, TILE)],
                out_sem.at[c % 2, 0],
            ),
            pltpu.make_async_copy(
                out_buf.at[c % 2, 0], first_out.at[pl.ds(c * TILE, TILE)], out_sem.at[c % 2, 1]
            ),
        )

    def finish(c):
        rs_copy(c).wait_recv()
        if c >= 2:
            for copy in out_copies(c - 2):
                copy.wait()
        total = project(c, 0) + part_recv[c].reshape(ROWS, WIDTH).astype(jnp.float32)
        out_buf[c % 2] = total.astype(jnp.bfloat16).reshape(FRAMES, TILE, WIDTH)
        for copy in out_copies(c):
            copy.start()

    for step in range(CHUNKS + 3):
        if step < CHUNKS:
            temporal(step)
        if 0 <= step - 1 < CHUNKS:
            share(step - 1)
        if 0 <= step - 2 < CHUNKS:
            partial(step - 2)
        if 0 <= step - 3 < CHUNKS:
            finish(step - 3)

    for c in range(CHUNKS):
        sent = send.at[c, pl.ds(0, SEQ - 1)]
        pltpu.make_async_copy(sent, sent, send_sem.at[c]).wait()
        sent = back.at[c, pl.ds(0, SEQ - 1)]
        pltpu.make_async_copy(sent, sent, back_send_sem.at[c]).wait()
        ag_copy(c).wait_send()
        rs_copy(c).wait_send()
    sp_copy.wait_send()
    for c in (CHUNKS - 2, CHUNKS - 1):
        for copy in out_copies(c):
            copy.wait()


def per_device(first_qkv, video_qkv, head_kind, out_weight):
    g = lax.axis_index("head")
    kinds = head_kind.reshape(4, LOCAL)
    orders = jnp.argsort(1 - kinds, axis=1, stable=True)
    order = lax.dynamic_index_in_dim(orders, g, 0, keepdims=False)
    first = first_qkv.reshape(3, 64, LOCAL, HEAD_DIM)
    kv = jnp.take(first[1:], order[:NS], axis=2).reshape(2, 64, SW)
    kv = lax.all_gather(kv, "seq", axis=1, tiled=True)
    rows = jnp.take(out_weight.reshape(LOCAL, HEAD_DIM, 96), order, axis=0).reshape(WIDTH, 96)
    rows = lax.all_gather(rows.T, "seq", axis=0, tiled=True)
    rows = lax.all_gather(rows, "head", axis=0).reshape(4, 4, WIDTH, WIDTH)

    def part(source, block):
        return lax.dynamic_slice(rows, (source, block, 0, 0), (1, 1, WIDTH, WIDTH))[0, 0]

    near = jnp.bitwise_xor(g, 1)
    weight = jnp.stack(
        [jnp.concatenate([part(g, b), part(near, b)], axis=1) for b in (g, 3 - g)]
    )
    bf16 = jnp.bfloat16
    any_spec = pl.BlockSpec(memory_space=pl.ANY)
    dma = pltpu.SemaphoreType.DMA
    first_out, video_out = pl.pallas_call(
        kernel,
        out_shape=(
            jax.ShapeDtypeStruct((64, WIDTH), bf16),
            jax.ShapeDtypeStruct((SEQ, 64, WIDTH), bf16),
        ),
        in_specs=[pl.BlockSpec(memory_space=pltpu.SMEM)] + [any_spec] * 4,
        out_specs=(any_spec, any_spec),
        scratch_shapes=[
            pltpu.VMEM((3, 64, WIDTH), bf16),
            pltpu.VMEM((2, 3, SEQ, TILE, WIDTH), bf16),
            pltpu.VMEM((3, NS, F, HEAD_DIM), bf16),
            pltpu.VMEM((2, F, SW), bf16),
            pltpu.VMEM((2, WIDTH, 2 * WIDTH), bf16),
            pltpu.VMEM((CHUNKS, SEQ, 3, TILE, TW), bf16),
            pltpu.VMEM((CHUNKS, FRAMES, 3, TILE, TW), bf16),
            pltpu.VMEM((CHUNKS, FRAMES, TILE, TW), bf16),
            pltpu.VMEM((CHUNKS, FRAMES, TILE, 2 * WIDTH), bf16),
            pltpu.VMEM((CHUNKS, FRAMES, TILE, WIDTH), bf16),
            pltpu.VMEM((CHUNKS, FRAMES, TILE, WIDTH), bf16),
            pltpu.VMEM((2, FRAMES, TILE, WIDTH), bf16),
            pltpu.VMEM((TILE, ROWS), jnp.float32),
            dma((2,)), dma((3,)), dma((CHUNKS,)), dma((CHUNKS,)), dma((CHUNKS,)), dma((CHUNKS,)),
            dma, dma, dma((CHUNKS,)), dma((CHUNKS,)), dma((CHUNKS,)), dma((CHUNKS,)), dma((2, 2)),
        ],
        compiler_params=pltpu.CompilerParams(
            collective_id=0, has_side_effects=True, vmem_limit_bytes=62 * 2**20
        ),
        name="denoise_attention",
    )(head_kind, first_qkv, video_qkv.reshape(3, SEQ, 64, WIDTH), kv, weight)
    return first_out, video_out.reshape(F, WIDTH)


def solution(mesh):
    in_specs = (P(None, "seq", "head"), P(None, "seq", "head"), P(), P("head", "seq"))
    out_specs = (P("seq", "head"), P("seq", "head"))
    return jax.shard_map(
        per_device, mesh=mesh, in_specs=in_specs, out_specs=out_specs, check_vma=False
    )
```

time: 490 us -> 483 us (0.986)
  Pallas kernels: 0 us -> 181 us
  local copies, waits for them, and re-layouts: 124 us -> 10.5 us
  matrix products: 51.7 us -> 0 us
  waiting for transfers between devices: 226 us -> 262 us
  starting transfers between devices: 34.7 us -> 0.12 us
  other arithmetic: 31 us -> 5.65 us
    all_gather x4 -> x3, waiting for transfers between devices: 35.9 us -> 262 us  [the longest x1 170 us: per_device(): rows = lax.all_gather(rows, 'head', axis=0).reshape(4, 4, WIDTH, WIDTH)]
    all_to_all x3 -> x0, waiting for transfers between devices: 189 us -> none  [the longest x1 97.4 us: per_device(): lax.all_to_all(weight_rows, 'head', split_axis=1, concat_axis=0, tiled=True)]
    pallas_call x0 -> x1, Pallas kernels: none -> 181 us  [per_device(): pl.pallas_call(kernel, out_shape=(jax.ShapeDtypeStruct((64, WIDTH), bf16)...]
    reshape x8 -> x1, local copies, waits for them, and re-layouts: 44.7 us -> 0.03 us  [per_device(): out_weight.reshape(LOCAL, HEAD_DIM, 96)]
    all_to_all x3 -> x0, starting transfers between devices: 34.1 us -> none  [the longest x1 20.2 us: per_device(): lax.all_to_all(leaving, 'seq', split_axis=0, concat_axis=1, tiled=True)]
    dot_general x9 -> x0, matrix products: 33.4 us -> none  [the longest x2 14.9 us: frame_attention(): jnp.einsum('hqk,khd->qhd', weights, value_rows, preferred_element_type=jn...]
    gather x10 -> x2, local copies, waits for them, and re-layouts: 30 us -> 1.14 us  [the longest x1 0.57 us: per_device(): jnp.take(out_weight.reshape(LOCAL, HEAD_DIM, 96), order, axis=0)]
    slice x15 -> x2, local copies, waits for them, and re-layouts: 19.1 us -> 0.15 us  [per_device(): kv = jnp.take(first[1:], order[:NS], axis=2).reshape(2, 64, SW)]
  transfers between devices with their start and end apart: 7 -> 3, of which waited for: 4 -> 3; matrix products, arithmetic and copies ran while one was open for 38% -> 1% of each run, Pallas kernels for 0% -> 0%
where the time goes in v1:
time: 483 us; the launch traced here: 474 us
  waiting for transfers between devices  262 us (54%)
  Pallas kernels  181 us (37%)
  between operations  13.8 us (3%)
  local copies, waits for them, and re-layouts  10.5 us (2%)
  other arithmetic  5.65 us (1%)
    pallas_call x1, Pallas kernels, per_device(): pl.pallas_call(kernel, out_shape=(jax.ShapeDtypeStruct((64, WIDTH), bf16)...  181 us
    all_gather x1, waiting for transfers between devices, per_device(): rows = lax.all_gather(rows, 'head', axis=0).reshape(4, 4, WIDTH, WIDTH)  170 us
    all_gather x1, waiting for transfers between devices, per_device(): rows = lax.all_gather(rows.T, 'seq', axis=0, tiled=True)  49.8 us
    all_gather x1, waiting for transfers between devices, per_device(): kv = lax.all_gather(kv, 'seq', axis=1, tiled=True)  42.4 us
  transfers between devices with their start and end apart: 3, of which 3 were waited for; matrix products, arithmetic and copies ran while one was open for 1% of the time, Pallas kernels for 0%

profile of v1, /device:TPU:2, one launch (start us, length us, event | category | flops | bytes accessed | tf_op | source)
XLA Modules:
  0.0 473.7 jit_solution(2992766635444704556)
XLA Ops:
  7.2 0.0 copy-start
  7.2 0.0 all-gather.7.cloned.1.call-start
  7.2 0.7 broadcast_subtract_fusion
  7.9 0.1 sub.10
  8.0 0.1 copy.11
  8.1 0.7 sort.17
  8.8 0.2 fusion.3
  9.0 0.0 copy-done
  9.0 0.1 broadcast_bitcast_fusion
  9.1 0.6 gather_fusion.1
  9.7 0.7 fusion
  10.4 0.0 all-gather.7.cloned.1.call-update
  10.4 0.0 all-gather.9.cloned.1.call-start
  10.4 49.8 %all-gather.7.cloned.1.call-done = bf16[3072,768]{1,0:T(8,128)(2,1)} async-done(((bf16[96,768]{1,0:T(8,128)(2,1)}), bf16[3072,768]{1,0:T(8,128)(2,1)}) %all-gather.7.cloned.1.call-update) | async-done | bytes 4718608 | tf_op jit(solution)/shard_map/all_gather | solution.py:294
  60.2 0.0 copy-start.1
  60.2 0.0 all-gather.9.cloned.1.call-update
  60.3 0.0 all-gather.5.cloned.1.call-start
  60.3 0.1 slice_reduce_fusion
  60.4 0.8 copy-done.1
  61.2 0.6 gather_fusion
  61.8 0.1 broadcast_bitcast_fusion.1
  61.9 0.6 bitcast_select_fusion.1
  62.5 0.0 all-gather.5.cloned.1.call-update
  62.6 170.1 %all-gather.9.cloned.1.call-done = bf16[12288,768]{1,0:T(8,128)(2,1)} async-done(((bf16[3072,768]{1,0:T(8,128)(2,1)}), bf16[12288,768]{1,0:T(8,128)(2,1)}) %all-gather.9.cloned.1.call-update) | async-done | bytes 18874384 | tf_op jit(solution)/shard_map/all_gather | solution.py:295
  232.7 2.6 dynamic-slice_bitcast_fusion.3
  235.3 0.4 maximum_bitcast_fusion
  235.7 2.5 pad_maximum_fusion.w_hbm
  238.2 42.4 %all-gather.5.cloned.1.call-done.kv_hbm = bf16[2,2048,256]{2,1,0:T(8,128)(2,1)} async-done(((bf16[2,64,256]{2,1,0:T(8,128)(2,1)}), bf16[2,2048,256]{2,1,0:T(8,128)(2,1)}) %all-gather.5.cloned.1.call-update) | async-done | bytes 2097168 | tf_op jit(solution)/shard_map/all_gather | solution.py:292
  280.6 181.2 %denoise_attention.1 = (bf16[64,768]{1,0:T(8,128)(2,1)}, bf16[32,64,768]{2,1,0:T(8,128)(2,1)}) custom-call(s32[24]{0:T(128)} %kinds.1, bf16[3,64,768]{2,1,0:T(8,128)(2,1)} %first_hbm.1, bf16[3,32,64,768]{3,2,1,0:T(8,128)(2,1)} %bitcast.52, bf16[2,2048,256]{2,1,0:T(8,128)(2,1)} %all-gather.5.cloned.1.call-done.kv_hbm, bf16[2,768,1536]{2,1,0:T(8,128)(2,1)} %pad_maximum_fusion.w_hbm), custom_call_target="tpu_custom_call" | custom-call | tf_op jit(solution)/shard_map/denoise_attention/pallas_call | solution.py:307
  461.9 1.5 copy.26
  463.4 3.8 copy.27
  (9 shorter events, 0.1 us)
Async XLA Ops:
  7.2 1.8 copy-start
  7.2 53.1 %all-gather.7.cloned.1.call-start = ((), (), s32[]{:S(2)}) async-start(), calls=%async_computation.1 | async-start | bytes 4866048 | tf_op jit(solution)/shard_map/all_gather | solution.py:294
  10.4 222.3 %all-gather.9.cloned.1.call-start = ((), (), s32[]{:S(2)}) async-start(), calls=%async_computation.2 | async-start | bytes 23592960 | tf_op jit(solution)/shard_map/all_gather | solution.py:295
  60.2 1.0 copy-start.1
  60.3 220.4 %all-gather.5.cloned.1.call-start = ((), (), s32[]{:S(2)}) async-start(), calls=%async_computation | async-start | bytes 2162688 | tf_op jit(solution)/shard_map/all_gather | solution.py:292
Sparse Core Ops, SparseCore 0:
  10.8 49.3 all-gather.6
  61.9 170.7 all-gather.8
  235.6 44.9 all-gather.4

commit v2 on v1

--- a/solution.py
+++ b/solution.py
@@ -19,6 +19,7 @@
 SW = NS * HEAD_DIM
 TW = NT * HEAD_DIM
 FRAMES = SEQ + 1
+SHARD = 96
 ROWS = FRAMES * TILE
 EXP_SCALE = HEAD_DIM ** (-0.5) * 1.4426950408889634
 MASKED = -1e30
@@ -27,15 +28,17 @@
 
 
 def kernel(
-    kinds, first_hbm, video_hbm, kv_hbm, w_hbm, first_out, video_out,
-    first, stage, spatial, kv, weight, send, recv, back, act, part_send, part_recv, out_buf, bias,
+    kinds, first_hbm, video_hbm, w_hbm, first_out, video_out,
+    first, stage, spatial, kv, shard_in, shard, weight, send, recv, back, act, part_send, part_recv, out_buf, bias,
     load_sem, const_sem, send_sem, recv_sem, back_send_sem, back_recv_sem,
     sp_send_sem, sp_recv_sem, ag_send_sem, ag_recv_sem, rs_send_sem, rs_recv_sem, out_sem,
+    swap_sem, kv_send_sem, kv_recv_sem, w_send_sem, w_recv_sem,
 ):
     s = lax.axis_index("seq")
     g = lax.axis_index("head")
     near = jnp.bitwise_xor(g, 1)
     far = 3 - g
+    y, z, core = s // 8, (s // 2) % 4, s % 2
 
     def load(c):
         return pltpu.make_async_copy(
@@ -46,10 +49,8 @@
     load(1).start()
     first_copy = pltpu.make_async_copy(first_hbm, first, const_sem.at[0])
     first_copy.start()
-    kv_copy = pltpu.make_async_copy(kv_hbm, kv, const_sem.at[1])
-    kv_copy.start()
-    w_copy = pltpu.make_async_copy(w_hbm, weight, const_sem.at[2])
-    w_copy.start()
+    shard_copy = pltpu.make_async_copy(w_hbm, shard_in, const_sem.at[1])
+    shard_copy.start()
 
     barrier = pltpu.get_barrier_semaphore()
 
@@ -100,10 +101,165 @@
             if plane == 0:
                 for slot in range(NS):
                     act[c, 0, :, slot * HEAD_DIM : (slot + 1) * HEAD_DIM] = pick(slot, heads)
+            else:
+                for slot in range(NS):
+                    kv[
+                        y, z, core, plane - 1, c * TILE : (c + 1) * TILE,
+                        slot * HEAD_DIM : (slot + 1) * HEAD_DIM,
+                    ] = pick(slot, heads)
+
+    shard_copy.wait()
+    for r in range(0, SHARD, TILE):
+        heads = split(shard_in[r : r + TILE, :])
+        for slot in range(LOCAL):
+            shard[r : r + TILE, slot * HEAD_DIM : (slot + 1) * HEAD_DIM] = pick(slot, heads)
+
+    def outer(n):
+        return jnp.logical_or(n == 0, n == 3)
+
+    stays = outer(y) == outer(g)
+    own_block = jnp.where(y == g, 0, 1)
+    near_block = jnp.where(y == near, 0, 1)
+    low, high = pl.ds(0, WIDTH), pl.ds(WIDTH, WIDTH)
+
+    def swap_copy(block):
+        return pltpu.make_async_remote_copy(
+            src_ref=shard, dst_ref=weight.at[block, z, core, :, high],
+            send_sem=swap_sem.at[0], recv_sem=swap_sem.at[1],
+            device_id=(s, near), device_id_type=MESH,
+        )
+
+    def to_seq(source, target, send_sem_, recv_sem_):
+        pltpu.make_async_remote_copy(
+            src_ref=source, dst_ref=source, send_sem=send_sem_, recv_sem=recv_sem_,
+            device_id=(target, g), device_id_type=MESH,
+        ).start()
+
+    def along_z(source, send_sem_, recv_sem_):
+        for k in range(1, 4):
+            to_seq(source, y * 8 + ((z + k) % 4) * 2 + core, send_sem_, recv_sem_)
+
+    def along_y(source, send_sem_, recv_sem_):
+        for k in range(1, 4):
+            to_seq(source, ((y + k) % 4) * 8 + z * 2 + core, send_sem_, recv_sem_)
+
+    def across(source, send_sem_, recv_sem_):
+        to_seq(source, s + 1 - 2 * core, send_sem_, recv_sem_)
+
+    def await_bytes(ref, sem):
+        pltpu.make_async_copy(ref, ref, sem).wait()
+
+    def swap_start():
+        @pl.when(jnp.logical_not(stays))
+        def _():
+            swap_copy(near_block).start()
+
+        @pl.when(stays)
+        def _():
+            weight[own_block, z, core, :, 0:WIDTH] = shard[...]
+
+    def kv_first():
+        @pl.when(core == 0)
+        def _():
+            along_z(kv.at[y, z, core], kv_send_sem.at[0], kv_recv_sem.at[0])
+
+        @pl.when(core == 1)
+        def _():
+            along_y(kv.at[y, z, core], kv_send_sem.at[0], kv_recv_sem.at[0])
+
+    def kv_second():
+        await_bytes(kv.at[y, pl.ds(0, 3), core], kv_recv_sem.at[0])
+
+        @pl.when(core == 0)
+        def _():
+            along_y(kv.at[y, :, core], kv_send_sem.at[1], kv_recv_sem.at[1])
+
+        @pl.when(core == 1)
+        def _():
+            along_z(kv.at[:, z, core], kv_send_sem.at[1], kv_recv_sem.at[1])
+
+    def kv_third():
+        await_bytes(kv.at[pl.ds(0, 3), :, core], kv_recv_sem.at[1])
+        across(kv.at[:, :, core], kv_send_sem.at[2], kv_recv_sem.at[2])
+
+    def w_first():
+        @pl.when(stays)
+        def _():
+            swap_copy(own_block).wait_recv()
+
+            @pl.when(core == 0)
+            def _():
+                along_z(weight.at[own_block, z, core], w_send_sem.at[0], w_recv_sem.at[0])
+
+            @pl.when(core == 1)
+            def _():
+                along_y(weight.at[own_block, z, core], w_send_sem.at[0], w_recv_sem.at[0])
+
+    def w_second():
+        @pl.when(core == 0)
+        def _():
+            @pl.when(stays)
+            def _():
+                await_bytes(weight.at[own_block, pl.ds(0, 3), core], w_recv_sem.at[0])
+                along_y(weight.at[own_block, :, core], w_send_sem.at[1], w_recv_sem.at[1])
+
+        @pl.when(core == 1)
+        def _():
+            @pl.when(stays)
+            def _():
+                await_bytes(weight.at[0, z, core], w_recv_sem.at[0])
+
+            @pl.when(jnp.logical_not(stays))
+            def _():
+                await_bytes(weight.at[:, z, core], w_recv_sem.at[0])
+
+            along_z(weight.at[:, z, core], w_send_sem.at[1], w_recv_sem.at[1])
+
+    def w_third():
+        @pl.when(core == 0)
+        def _():
+            @pl.when(stays)
+            def _():
+                await_bytes(weight.at[0, :, core], w_recv_sem.at[1])
+
+            @pl.when(jnp.logical_not(stays))
+            def _():
+                await_bytes(weight.at[:, :, core], w_recv_sem.at[1])
+
+        @pl.when(core == 1)
+        def _():
+            await_bytes(weight.at[:, pl.ds(0, 3), core], w_recv_sem.at[1])
+
+        across(weight.at[:, :, core], w_send_sem.at[2], w_recv_sem.at[2])
+
+    def spread_sent():
+        await_bytes(kv.at[0, pl.ds(0, 3), core], kv_send_sem.at[0])
+        await_bytes(kv.at[pl.ds(0, 3), :, core], kv_send_sem.at[1])
+        await_bytes(kv.at[:, :, core], kv_send_sem.at[2])
+        await_bytes(weight.at[:, :, core], w_send_sem.at[2])
+
+        @pl.when(jnp.logical_not(stays))
+        def _():
+            swap_copy(near_block).wait_send()
+
+        @pl.when(stays)
+        def _():
+            await_bytes(weight.at[0, pl.ds(0, 3), core], w_send_sem.at[0])
+
+        @pl.when(jnp.logical_and(stays, core == 0))
+        def _():
+            for _k in range(3):
+                await_bytes(weight.at[0, :, core], w_send_sem.at[1])
+
+        @pl.when(core == 1)
+        def _():
+            await_bytes(weight.at[:, pl.ds(0, 3), core], w_send_sem.at[1])
 
     pl.semaphore_wait(barrier, SEQ + 1)
-
-    for c in range(CHUNKS):
+    swap_start()
+    kv_first()
+
+    def pack_and_post(c):
         load(c).wait()
 
         def pack(d, carry):
@@ -134,6 +290,13 @@
         lax.fori_loop(1, SEQ, post, 0)
         pltpu.make_async_copy(send.at[c, s], recv.at[c, 1 + s], recv_sem.at[c]).start()
 
+    pack_and_post(0)
+    pack_and_post(1)
+    w_first()
+    kv_second()
+    pack_and_post(2)
+    pack_and_post(3)
+
     def attend(q, k, v, mask):
         scores = lax.dot_general(q, k, NT_DIMS, preferred_element_type=jnp.float32)
         if mask is not None:
@@ -158,12 +321,22 @@
             return carry
 
         lax.fori_loop(0, F // block, frame_block, 0)
-
-    kv_copy.wait()
+        if h == 0:
+            w_second()
+            kv_third()
+        else:
+            w_third()
+
+    await_bytes(kv.at[:, :, core], kv_recv_sem.at[2])
     for h in range(NS):
         columns = slice(h * HEAD_DIM, (h + 1) * HEAD_DIM)
         queries = act[:, 0, :, columns].reshape(CHUNKS * TILE, HEAD_DIM)
-        mixed = attend(queries, kv[0, :, columns], kv[1, :, columns], None)
+        mixed = attend(
+            queries,
+            kv[:, :, :, 0, :, columns].reshape(F, HEAD_DIM),
+            kv[:, :, :, 1, :, columns].reshape(F, HEAD_DIM),
+            None,
+        )
         for c in range(CHUNKS):
             act[c, 0, :, columns] = mixed[c * TILE : (c + 1) * TILE]
 
@@ -226,14 +399,14 @@
 
     def project(c, which):
         return lax.dot_general(
-            act[c].reshape(ROWS, 2 * WIDTH), weight[which], NT_DIMS,
+            act[c].reshape(ROWS, 2 * WIDTH), weight[which].reshape(WIDTH, 2 * WIDTH), NT_DIMS,
             preferred_element_type=jnp.float32,
         )
 
     def partial(c):
         if c == 0:
             sp_copy.wait_recv()
-            w_copy.wait()
+            await_bytes(weight.at[:, :, core], w_recv_sem.at[2])
         ag_copy(c).wait_recv()
         part_send[c] = project(c, 1).astype(jnp.bfloat16).reshape(FRAMES, TILE, WIDTH)
         rs_copy(c).start()
@@ -277,30 +450,13 @@
         ag_copy(c).wait_send()
         rs_copy(c).wait_send()
     sp_copy.wait_send()
+    spread_sent()
     for c in (CHUNKS - 2, CHUNKS - 1):
         for copy in out_copies(c):
             copy.wait()
 
 
 def per_device(first_qkv, video_qkv, head_kind, out_weight):
-    g = lax.axis_index("head")
-    kinds = head_kind.reshape(4, LOCAL)
-    orders = jnp.argsort(1 - kinds, axis=1, stable=True)
-    order = lax.dynamic_index_in_dim(orders, g, 0, keepdims=False)
-    first = first_qkv.reshape(3, 64, LOCAL, HEAD_DIM)
-    kv = jnp.take(first[1:], order[:NS], axis=2).reshape(2, 64, SW)
-    kv = lax.all_gather(kv, "seq", axis=1, tiled=True)
-    rows = jnp.take(out_weight.reshape(LOCAL, HEAD_DIM, 96), order, axis=0).reshape(WIDTH, 96)
-    rows = lax.all_gather(rows.T, "seq", axis=0, tiled=True)
-    rows = lax.all_gather(rows, "head", axis=0).reshape(4, 4, WIDTH, WIDTH)
-
-    def part(source, block):
-        return lax.dynamic_slice(rows, (source, block, 0, 0), (1, 1, WIDTH, WIDTH))[0, 0]
-
-    near = jnp.bitwise_xor(g, 1)
-    weight = jnp.stack(
-        [jnp.concatenate([part(g, b), part(near, b)], axis=1) for b in (g, 3 - g)]
-    )
     bf16 = jnp.bfloat16
     any_spec = pl.BlockSpec(memory_space=pl.ANY)
     dma = pltpu.SemaphoreType.DMA
@@ -310,14 +466,16 @@
             jax.ShapeDtypeStruct((64, WIDTH), bf16),
             jax.ShapeDtypeStruct((SEQ, 64, WIDTH), bf16),
         ),
-        in_specs=[pl.BlockSpec(memory_space=pltpu.SMEM)] + [any_spec] * 4,
+        in_specs=[pl.BlockSpec(memory_space=pltpu.SMEM)] + [any_spec] * 3,
         out_specs=(any_spec, any_spec),
         scratch_shapes=[
             pltpu.VMEM((3, 64, WIDTH), bf16),
             pltpu.VMEM((2, 3, SEQ, TILE, WIDTH), bf16),
             pltpu.VMEM((3, NS, F, HEAD_DIM), bf16),
-            pltpu.VMEM((2, F, SW), bf16),
-            pltpu.VMEM((2, WIDTH, 2 * WIDTH), bf16),
+            pltpu.VMEM((4, 4, 2, 2, 64, SW), bf16),
+            pltpu.VMEM((SHARD, WIDTH), bf16),
+            pltpu.VMEM((SHARD, WIDTH), bf16),
+            pltpu.VMEM((2, 4, 2, SHARD, 2 * WIDTH), bf16),
             pltpu.VMEM((CHUNKS, SEQ, 3, TILE, TW), bf16),
             pltpu.VMEM((CHUNKS, FRAMES, 3, TILE, TW), bf16),
             pltpu.VMEM((CHUNKS, FRAMES, TILE, TW), bf16),
@@ -326,14 +484,15 @@
             pltpu.VMEM((CHUNKS, FRAMES, TILE, WIDTH), bf16),
             pltpu.VMEM((2, FRAMES, TILE, WIDTH), bf16),
             pltpu.VMEM((TILE, ROWS), jnp.float32),
-            dma((2,)), dma((3,)), dma((CHUNKS,)), dma((CHUNKS,)), dma((CHUNKS,)), dma((CHUNKS,)),
+            dma((2,)), dma((2,)), dma((CHUNKS,)), dma((CHUNKS,)), dma((CHUNKS,)), dma((CHUNKS,)),
             dma, dma, dma((CHUNKS,)), dma((CHUNKS,)), dma((CHUNKS,)), dma((CHUNKS,)), dma((2, 2)),
+            dma((2,)), dma((3,)), dma((3,)), dma((3,)), dma((3,)),
         ],
         compiler_params=pltpu.CompilerParams(
             collective_id=0, has_side_effects=True, vmem_limit_bytes=62 * 2**20
         ),
         name="denoise_attention",
-    )(head_kind, first_qkv, video_qkv.reshape(3, SEQ, 64, WIDTH), kv, weight)
+    )(head_kind, first_qkv, video_qkv.reshape(3, SEQ, 64, WIDTH), out_weight.T)
     return first_out, video_out.reshape(F, WIDTH)
 
 

time: 483 us -> 243 us (0.50); the launches traced: 474 us -> 243 us
  waiting for transfers between devices: 262 us -> 0 us
  Pallas kernels: 181 us -> 237 us
  between operations: 13.8 us -> 0.64 us
  other arithmetic: 5.65 us -> 0 us
  local copies, waits for them, and re-layouts: 10.5 us -> 5.29 us
    all_gather x3 -> x0, waiting for transfers between devices: 262 us -> none  [the longest x1 170 us: per_device(): rows = lax.all_gather(rows, 'head', axis=0).reshape(4, 4, WIDTH, WIDTH)]
    pallas_call x1, Pallas kernels: 181 us -> 237 us  [per_device(): pl.pallas_call(kernel, out_shape=(jax.ShapeDtypeStruct((64, WIDTH), bf16)...]
  transfers between devices with their start and end apart: 3 -> 0, of which waited for: 3 -> 0; matrix products, arithmetic and copies ran while one was open for 1% -> 0% of each run, Pallas kernels for 0% -> 0%
where the time goes in v2:
time: 243 us
  Pallas kernels  237 us (98%)
  local copies, waits for them, and re-layouts  5.29 us (2%)
    pallas_call x1, Pallas kernels, per_device(): pl.pallas_call(kernel, out_shape=(jax.ShapeDtypeStruct((64, WIDTH), bf16)...  237 us
    unnamed x2, local copies, waits for them, and re-layouts  5.29 us

profile of v2, /device:TPU:2, one launch (start us, length us, event | category | flops | bytes accessed | tf_op | source)
XLA Modules:
  0.0 243.0 jit_solution(17465747004008712416)
XLA Ops:
  0.6 237.1 %denoise_attention.1 = (bf16[64,768]{1,0:T(8,128)(2,1)}, bf16[32,64,768]{2,1,0:T(8,128)(2,1)}) custom-call(s32[24]{0:T(128)} %kinds.1, bf16[3,64,768]{2,1,0:T(8,128)(2,1)} %first_hbm.1, bf16[3,32,64,768]{3,2,1,0:T(8,128)(2,1)} %bitcast.3, bf16[96,768]{1,0:T(8,128)(2,1)} %bitcast.5), custom_call_target="tpu_custom_call" | custom-call | tf_op jit(solution)/shard_map/denoise_attention/pallas_call | solution.py:463
  237.7 1.5 copy.8
  239.2 3.8 %copy.9 = bf16[2048,768]{1,0:T(8,128)(2,1)} copy(bf16[2048,768]{1,0:T(8,128)(2,1)} %bitcast.4) | data formatting | bytes 6291456

commit v3 on v1

v3 whole, which is shorter than its diff:
```python
import functools

import jax
import jax.numpy as jnp
from jax import lax
from jax.experimental import pallas as pl
from jax.experimental.pallas import tpu as pltpu
from jax.sharding import PartitionSpec as P

HEAD_DIM = 128
F = 2048
SEQ = 32
LOCAL = 6
NS = 2
NT = 4
PAIRS = 4
CHUNKS = 2 * PAIRS
TILE = 16
HALF = 8
WIDTH = LOCAL * HEAD_DIM
SW = NS * HEAD_DIM
TW = 2 * HEAD_DIM
FRAMES = SEQ + 1
SHARD = 96
ROWS = FRAMES * TILE
HALF_ROWS = FRAMES * HALF
EXP_SCALE = HEAD_DIM ** (-0.5) * 1.4426950408889634
MASKED = -1e30
MESH = pl.DeviceIdType.MESH
NT_DIMS = (((1,), (1,)), ((), ()))


def kernel(
    kinds, first_hbm, video_hbm, w_hbm, first_out, video_out,
    first, stage, spatial, kv, shard_in, shard, weight, send, recv, back, own_s, near_s, own_t, near_t,
    part_send, part_recv, acc, out_buf, bias,
    load_sem, const_sem, send_sem, recv_sem, back_send_sem, back_recv_sem,
    sp_send_sem, sp_recv_sem, ag_send_sem, ag_recv_sem, rs_send_sem, rs_recv_sem, out_sem,
    swap_sem, kv_send_sem, kv_recv_sem, w_send_sem, w_recv_sem,
):
    s = lax.axis_index("seq")
    g = lax.axis_index("head")
    near = jnp.bitwise_xor(g, 1)
    far = 3 - g
    y, z, core = s // 8, (s // 2) % 4, s % 2

    def load(c):
        return pltpu.make_async_copy(
            video_hbm.at[:, :, pl.ds(c * TILE, TILE)], stage.at[c % 2], load_sem.at[c % 2]
        )

    load(0).start()
    load(1).start()
    first_copy = pltpu.make_async_copy(first_hbm, first, const_sem.at[0])
    first_copy.start()
    shard_copy = pltpu.make_async_copy(w_hbm, shard_in, const_sem.at[1])
    shard_copy.start()

    barrier = pltpu.get_barrier_semaphore()

    def greet(k, carry):
        pl.semaphore_signal(
            barrier, inc=1, device_id=(jnp.bitwise_xor(s, k), g), device_id_type=MESH
        )
        return carry

    lax.fori_loop(1, SEQ, greet, 0)
    mirror = jnp.bitwise_xor(y, 1)
    mirror_seq = mirror * 8 + z * 2 + core
    for other in ((s, near), (s, far), (mirror_seq, near)):
        pl.semaphore_signal(barrier, inc=1, device_id=other, device_id_type=MESH)

    kind = [kinds[g * LOCAL + h] for h in range(LOCAL)]
    takes = []
    for slot in range(LOCAL):
        want, rank = (1, slot) if slot < NS else (0, slot - NS)
        seen = jnp.int32(0)
        row = []
        for h in range(LOCAL):
            is_kind = kind[h] == want
            row.append(jnp.logical_and(is_kind, seen == rank))
            seen = seen + jnp.where(is_kind, 1, 0)
        takes.append(row)

    def pick(slot, heads):
        low, count = (slot, 5) if slot < NS else (slot - NS, 3)
        value = heads[low]
        for h in range(low + 1, low + count):
            value = lax.select(takes[slot][h], heads[h], value)
        return value

    f32, bf16 = jnp.float32, jnp.bfloat16

    def pack_tiles(heads):
        tiles = [pick(NS + slot, heads).astype(f32) for slot in range(NT)]
        packed = []
        for half in range(2):
            rows = slice(half * HALF, (half + 1) * HALF)
            sides = [jnp.concatenate([tiles[i][rows], tiles[i + 2][rows]], axis=0) for i in range(2)]
            packed.append(jnp.concatenate(sides, axis=1).astype(bf16))
        return packed

    def split(tile):
        return [tile[:, h * HEAD_DIM : (h + 1) * HEAD_DIM] for h in range(LOCAL)]

    row_id = lax.broadcasted_iota(jnp.int32, (TILE, ROWS), 0)
    col_id = lax.broadcasted_iota(jnp.int32, (TILE, ROWS), 1)
    bias[...] = jnp.where(row_id == jnp.bitwise_and(col_id, TILE - 1), 0.0, MASKED)

    first_copy.wait()
    for c in range(PAIRS):
        for plane in range(3):
            heads = split(first[plane, c * TILE : (c + 1) * TILE, :])
            for half, tile in enumerate(pack_tiles(heads)):
                recv[2 * c + half, 0, plane] = tile
            if plane == 0:
                for slot in range(NS):
                    own_s[c, 0, :, slot * HEAD_DIM : (slot + 1) * HEAD_DIM] = pick(slot, heads)
            else:
                for slot in range(NS):
                    kv[
                        y, z, core, plane - 1, c * TILE : (c + 1) * TILE,
                        slot * HEAD_DIM : (slot + 1) * HEAD_DIM,
                    ] = pick(slot, heads)

    shard_copy.wait()
    for r in range(0, SHARD, TILE):
        heads = split(shard_in[r : r + TILE, :])
        for slot in range(LOCAL):
            shard[r : r + TILE, slot * HEAD_DIM : (slot + 1) * HEAD_DIM] = pick(slot, heads)

    def outer(n):
        return jnp.logical_or(n == 0, n == 3)

    stays = outer(y) == outer(g)
    swap_copy = pltpu.make_async_remote_copy(
        src_ref=shard, dst_ref=weight.at[mirror, z, core],
        send_sem=swap_sem.at[0], recv_sem=swap_sem.at[1],
        device_id=(mirror_seq, near), device_id_type=MESH,
    )

    def swap_start():
        @pl.when(jnp.logical_not(stays))
        def _():
            swap_copy.start()

        @pl.when(stays)
        def _():
            weight[y, z, core] = shard[...]

    def swap_wait():
        @pl.when(jnp.logical_not(stays))
        def _():
            swap_copy.wait()

    def to_seq(ref, target, sems):
        pltpu.make_async_remote_copy(
            src_ref=ref, dst_ref=ref, send_sem=sems[0], recv_sem=sems[1],
            device_id=(target, g), device_id_type=MESH,
        ).start()

    def along_z(ref, sems):
        for k in range(1, 4):
            to_seq(ref, y * 8 + ((z + k) % 4) * 2 + core, sems)

    def along_y(ref, sems):
        for k in range(1, 4):
            to_seq(ref, ((y + k) % 4) * 8 + z * 2 + core, sems)

    def await_bytes(ref, sem):
        pltpu.make_async_copy(ref, ref, sem).wait()

    class Spread:
        def __init__(self, buf, send_sems, recv_sems):
            self.buf = buf
            self.sems = [(send_sems.at[i], recv_sems.at[i]) for i in range(3)]

        def first(self):
            @pl.when(core == 0)
            def _():
                along_z(self.buf.at[y, z, core], self.sems[0])

            @pl.when(core == 1)
            def _():
                along_y(self.buf.at[y, z, core], self.sems[0])

        def second(self):
            await_bytes(self.buf.at[0, pl.ds(0, 3), core], self.sems[0][1])

            @pl.when(core == 0)
            def _():
                along_y(self.buf.at[y, :, core], self.sems[1])

            @pl.when(core == 1)
            def _():
                along_z(self.buf.at[:, z, core], self.sems[1])

        def third(self):
            await_bytes(self.buf.at[pl.ds(0, 3), :, core], self.sems[1][1])
            to_seq(self.buf.at[:, :, core], s + 1 - 2 * core, self.sems[2])

        def arrived(self):
            await_bytes(self.buf.at[:, :, core], self.sems[2][1])

        def sent(self):
            await_bytes(self.buf.at[0, pl.ds(0, 3), core], self.sems[0][0])
            await_bytes(self.buf.at[pl.ds(0, 3), :, core], self.sems[1][0])
            await_bytes(self.buf.at[:, :, core], self.sems[2][0])

    kv_spread = Spread(kv, kv_send_sem, kv_recv_sem)
    w_spread = Spread(weight, w_send_sem, w_recv_sem)


    def pack_chunk(c):
        load(c).wait()

        def pack(d, carry):
            for plane in range(3):
                heads = split(stage[c % 2, plane, d])
                for half, tile in enumerate(pack_tiles(heads)):
                    send[2 * c + half, d, plane] = tile
                start = pl.multiple_of(d * (PAIRS * TILE) + c * TILE, TILE)
                for slot in range(NS):
                    spatial[plane, slot, pl.ds(start, TILE), :] = pick(slot, heads)
            return carry

        lax.fori_loop(0, SEQ, pack, 0)
        if c + 2 < PAIRS:
            load(c + 2).start()

    def peer(i):
        bits = (i % 2) * 16 + ((i // 2) % 2) * 8 + ((i // 4) % 2) * 4 + ((i // 8) % 2) * 2 + i // 16
        return jnp.bitwise_xor(s, bits)

    def post_chunk(c):
        def post(i, carry):
            d = peer(i)
            pltpu.make_async_remote_copy(
                src_ref=send.at[c, d], dst_ref=recv.at[c, 1 + s],
                send_sem=send_sem.at[c], recv_sem=recv_sem.at[c],
                device_id=(d, g), device_id_type=MESH,
            ).start()
            return carry

        lax.fori_loop(1, SEQ, post, 0)
        pltpu.make_async_copy(send.at[c, s], recv.at[c, 1 + s], recv_sem.at[c]).start()

    def attend(q, k, v, mask):
        scores = lax.dot_general(q, k, NT_DIMS, preferred_element_type=jnp.float32)
        if mask is not None:
            scores = (scores.reshape(FRAMES, TILE, ROWS) + mask[None]).reshape(ROWS, ROWS)
        top = jnp.max(scores, axis=-1, keepdims=True)
        raised = jnp.exp2((scores - top) * EXP_SCALE)
        total = jnp.sum(raised, axis=-1, keepdims=True)
        mixed = jnp.dot(raised.astype(jnp.bfloat16), v, preferred_element_type=jnp.float32)
        return (mixed / total).astype(jnp.bfloat16)

    def sp_copy(h):
        return pltpu.make_async_remote_copy(
            src_ref=own_s.at[:, pl.ds(1, SEQ), :, pl.ds(h * HEAD_DIM, HEAD_DIM)],
            dst_ref=near_s.at[:, pl.ds(1, SEQ), :, pl.ds(h * HEAD_DIM, HEAD_DIM)],
            send_sem=sp_send_sem.at[h], recv_sem=sp_recv_sem.at[h],
            device_id=(s, near), device_id_type=MESH,
        )

    first_share = pltpu.make_async_remote_copy(
        src_ref=own_s.at[:, 0], dst_ref=near_s.at[:, 0],
        send_sem=sp_send_sem.at[NS], recv_sem=sp_recv_sem.at[NS],
        device_id=(s, near), device_id_type=MESH,
    )

    block = 256

    def frame_head(h):
        columns = slice(h * HEAD_DIM, (h + 1) * HEAD_DIM)
        owners = block // (PAIRS * TILE)

        def frame_block(b, carry):
            start = pl.multiple_of(b * block, block)
            mixed = attend(spatial[0, h, pl.ds(start, block), :], spatial[1, h], spatial[2, h], None)
            for dd in range(owners):
                for c in range(PAIRS):
                    at = (dd * PAIRS + c) * TILE
                    own_s[c, 1 + b * owners + dd, :, columns] = mixed[at : at + TILE]
            return carry

        lax.fori_loop(0, F // block, frame_block, 0)
        sp_copy(h).start()

    def first_frame():
        kv_spread.arrived()
        for h in range(NS):
            columns = slice(h * HEAD_DIM, (h + 1) * HEAD_DIM)
            queries = own_s[:, 0, :, columns].reshape(PAIRS * TILE, HEAD_DIM)
            mixed = attend(
                queries,
                kv[:, :, :, 0, :, columns].reshape(F, HEAD_DIM),
                kv[:, :, :, 1, :, columns].reshape(F, HEAD_DIM),
                None,
            )
            for c in range(PAIRS):
                own_s[c, 0, :, columns] = mixed[c * TILE : (c + 1) * TILE]
        first_share.start()

    def temporal(c):
        pltpu.make_async_copy(
            recv.at[c, pl.ds(1, SEQ)], recv.at[c, pl.ds(1, SEQ)], recv_sem.at[c]
        ).wait()

        def one_head(t, carry):
            columns = pl.ds(pl.multiple_of(t * HEAD_DIM, HEAD_DIM), HEAD_DIM)
            q, k, v = (
                recv[c, :, plane, :, columns].reshape(ROWS, HEAD_DIM) for plane in range(3)
            )
            mixed = attend(q, k, v, bias[...])
            back[c, :, :, columns] = mixed.reshape(FRAMES, TILE, HEAD_DIM)
            return carry

        lax.fori_loop(0, 2, one_head, 0)

        def post(i, carry):
            d = peer(i)
            pltpu.make_async_remote_copy(
                src_ref=back.at[c, 1 + d], dst_ref=own_t.at[c, 1 + s],
                send_sem=back_send_sem.at[c], recv_sem=back_recv_sem.at[c],
                device_id=(d, g), device_id_type=MESH,
            ).start()
            return carry

        lax.fori_loop(1, SEQ, post, 0)
        pltpu.make_async_copy(
            back.at[c, 1 + s], own_t.at[c, 1 + s], back_recv_sem.at[c]
        ).start()
        own_t[c, 0] = back[c, 0]

    def ag_copy(c):
        return pltpu.make_async_remote_copy(
            src_ref=own_t.at[c], dst_ref=near_t.at[c],
            send_sem=ag_send_sem.at[c], recv_sem=ag_recv_sem.at[c],
            device_id=(s, near), device_id_type=MESH,
        )

    def share(c):
        landed = own_t.at[c, pl.ds(1, SEQ)]
        pltpu.make_async_copy(landed, landed, back_recv_sem.at[c]).wait()
        ag_copy(c).start()

    def rs_copy(c):
        return pltpu.make_async_remote_copy(
            src_ref=part_send.at[c], dst_ref=part_recv.at[c],
            send_sem=rs_send_sem.at[c], recv_sem=rs_recv_sem.at[c],
            device_id=(s, far), device_id_type=MESH,
        )

    def times(own, near_half, block):
        return sum(
            lax.dot_general(
                part.reshape(-1, WIDTH).astype(bf16), weight[at].reshape(WIDTH, WIDTH), NT_DIMS,
                preferred_element_type=f32,
            )
            for part, at in ((own, block), (near_half, jnp.bitwise_xor(block, 1)))
        )

    def half_rows(c, spatial_ref, temporal_ref):
        rows = slice((c % 2) * HALF, (c % 2 + 1) * HALF)
        mixed = temporal_ref[c].astype(f32)
        return jnp.concatenate(
            [spatial_ref[c // 2].astype(f32)[:, rows], mixed[:, :HALF], mixed[:, HALF:]], axis=2
        )

    def pair_rows(c, spatial_ref, temporal_ref):
        halves = [temporal_ref[2 * c + half].astype(f32) for half in range(2)]
        sides = [
            jnp.concatenate([half[:, rows] for half in halves], axis=1).astype(bf16)
            for rows in (slice(0, HALF), slice(HALF, TILE))
        ]
        return jnp.concatenate([spatial_ref[c]] + sides, axis=2)

    def partial(c):
        if c == 0:
            for h in range(NS):
                sp_copy(h).wait_recv()
            first_share.wait_recv()
            w_spread.arrived()
        ag_copy(c).wait_recv()
        part = times(half_rows(c, own_s, own_t), half_rows(c, near_s, near_t), far)
        part = part.reshape(FRAMES, HALF, WIDTH)
        part_send[c] = jnp.concatenate(
            [part[:, :, : WIDTH // 2], part[:, :, WIDTH // 2 :]], axis=1
        ).astype(bf16)
        rs_copy(c).start()

    def own_block(c):
        acc[...] = times(pair_rows(c, own_s, own_t), pair_rows(c, near_s, near_t), g).reshape(
            FRAMES, TILE, WIDTH
        )

    def out_copies(c):
        return (
            pltpu.make_async_copy(
                out_buf.at[c % 2, pl.ds(1, SEQ)], video_out.at[:, pl.ds(c * TILE, TILE)],
                out_sem.at[c % 2, 0],
            ),
            pltpu.make_async_copy(
                out_buf.at[c % 2, 0], first_out.at[pl.ds(c * TILE, TILE)], out_sem.at[c % 2, 1]
            ),
        )

    def finish(c):
        if c >= 2:
            for copy in out_copies(c - 2):
                copy.wait()
        halves = []
        for half in range(2):
            rs_copy(2 * c + half).wait_recv()
            part = part_recv[2 * c + half].astype(f32)
            halves.append(jnp.concatenate([part[:, :HALF], part[:, HALF:]], axis=2))
        out_buf[c % 2] = (acc[...] + jnp.concatenate(halves, axis=1)).astype(bf16)
        for copy in out_copies(c):
            copy.start()

    pack_chunk(0)
    pl.semaphore_wait(barrier, SEQ + 2)
    swap_start()
    kv_spread.first()
    post_chunk(0)
    swap_wait()
    w_spread.first()
    kv_spread.second()
    post_chunk(1)
    pack_chunk(1)
    pack_chunk(2)
    pack_chunk(3)
    w_spread.second()
    frame_head(0)
    temporal(0)
    post_chunk(2)
    kv_spread.third()
    frame_head(1)
    temporal(1)
    post_chunk(3)
    first_frame()
    w_spread.third()
    for step in range(2, CHUNKS):
        share(step - 2)
        temporal(step)
        if step + 2 < CHUNKS:
            post_chunk(step + 2)
        if step == CHUNKS - 1:
            share(CHUNKS - 2)
        partial(step - 2)
        if step == CHUNKS - 1:
            share(CHUNKS - 1)
        if step % 2 == 1:
            own_block((step - 3) // 2)
        elif step >= 4:
            finish((step - 4) // 2)
    partial(CHUNKS - 2)
    finish(PAIRS - 2)
    partial(CHUNKS - 1)
    own_block(PAIRS - 1)
    finish(PAIRS - 1)

    for c in range(CHUNKS):
        sent = send.at[c, pl.ds(0, SEQ - 1)]
        pltpu.make_async_copy(sent, sent, send_sem.at[c]).wait()
        sent = back.at[c, pl.ds(0, SEQ - 1)]
        pltpu.make_async_copy(sent, sent, back_send_sem.at[c]).wait()
        ag_copy(c).wait_send()
        rs_copy(c).wait_send()
    for h in range(NS):
        sp_copy(h).wait_send()
    first_share.wait_send()
    kv_spread.sent()
    w_spread.sent()
    for c in (PAIRS - 2, PAIRS - 1):
        for copy in out_copies(c):
            copy.wait()


def per_device(first_qkv, video_qkv, head_kind, out_weight):
    bf16 = jnp.bfloat16
    any_spec = pl.BlockSpec(memory_space=pl.ANY)
    dma = pltpu.SemaphoreType.DMA
    first_out, video_out = pl.pallas_call(
        kernel,
        out_shape=(
            jax.ShapeDtypeStruct((64, WIDTH), bf16),
            jax.ShapeDtypeStruct((SEQ, 64, WIDTH), bf16),
        ),
        in_specs=[pl.BlockSpec(memory_space=pltpu.SMEM)] + [any_spec] * 3,
        out_specs=(any_spec, any_spec),
        scratch_shapes=[
            pltpu.VMEM((3, 64, WIDTH), bf16),
            pltpu.VMEM((2, 3, SEQ, TILE, WIDTH), bf16),
            pltpu.VMEM((3, NS, F, HEAD_DIM), bf16),
            pltpu.VMEM((4, 4, 2, 2, 64, SW), bf16),
            pltpu.VMEM((SHARD, WIDTH), bf16),
            pltpu.VMEM((SHARD, WIDTH), bf16),
            pltpu.VMEM((4, 4, 2, SHARD, WIDTH), bf16),
            pltpu.VMEM((CHUNKS, SEQ, 3, TILE, TW), bf16),
            pltpu.VMEM((CHUNKS, FRAMES, 3, TILE, TW), bf16),
            pltpu.VMEM((CHUNKS, FRAMES, TILE, TW), bf16),
            pltpu.VMEM((PAIRS, FRAMES, TILE, SW), bf16),
            pltpu.VMEM((PAIRS, FRAMES, TILE, SW), bf16),
            pltpu.VMEM((CHUNKS, FRAMES, TILE, TW), bf16),
            pltpu.VMEM((CHUNKS, FRAMES, TILE, TW), bf16),
            pltpu.VMEM((CHUNKS, FRAMES, TILE, WIDTH // 2), bf16),
            pltpu.VMEM((CHUNKS, FRAMES, TILE, WIDTH // 2), bf16),
            pltpu.VMEM((FRAMES, TILE, WIDTH), jnp.float32),
            pltpu.VMEM((2, FRAMES, TILE, WIDTH), bf16),
            pltpu.VMEM((TILE, ROWS), jnp.float32),
            dma((2,)), dma((2,)), dma((CHUNKS,)), dma((CHUNKS,)), dma((CHUNKS,)), dma((CHUNKS,)),
            dma((NS + 1,)), dma((NS + 1,)), dma((CHUNKS,)), dma((CHUNKS,)), dma((CHUNKS,)), dma((CHUNKS,)), dma((2, 2)),
            dma((2,)), dma((3,)), dma((3,)), dma((3,)), dma((3,)),
        ],
        compiler_params=pltpu.CompilerParams(
            collective_id=0, has_side_effects=True, vmem_limit_bytes=62 * 2**20
        ),
        name="denoise_attention",
    )(head_kind, first_qkv, video_qkv.reshape(3, SEQ, 64, WIDTH), out_weight.T)
    return first_out, video_out.reshape(F, WIDTH)


def solution(mesh):
    in_specs = (P(None, "seq", "head"), P(None, "seq", "head"), P(), P("head", "seq"))
    out_specs = (P("seq", "head"), P("seq", "head"))
    return jax.shard_map(
        per_device, mesh=mesh, in_specs=in_specs, out_specs=out_specs, check_vma=False
    )
```

time: 483 us -> 165 us (0.34); the launches traced: 474 us -> 163 us
  waiting for transfers between devices: 262 us -> 0 us
  Pallas kernels: 181 us -> 157 us
  between operations: 13.8 us -> 0.64 us
  other arithmetic: 5.65 us -> 0 us
  local copies, waits for them, and re-layouts: 10.5 us -> 5.29 us
    all_gather x3 -> x0, waiting for transfers between devices: 262 us -> none  [the longest x1 170 us: per_device(): rows = lax.all_gather(rows, 'head', axis=0).reshape(4, 4, WIDTH, WIDTH)]
    pallas_call x1, Pallas kernels: 181 us -> 157 us  [per_device(): pl.pallas_call(kernel, out_shape=(jax.ShapeDtypeStruct((64, WIDTH), bf16)...]
  transfers between devices with their start and end apart: 3 -> 0, of which waited for: 3 -> 0; matrix products, arithmetic and copies ran while one was open for 1% -> 0% of each run, Pallas kernels for 0% -> 0%
where the time goes in v3:
time: 165 us; the launch traced here: 163 us
  Pallas kernels  157 us (95%)
  local copies, waits for them, and re-layouts  5.29 us (3%)
    pallas_call x1, Pallas kernels, per_device(): pl.pallas_call(kernel, out_shape=(jax.ShapeDtypeStruct((64, WIDTH), bf16)...  157 us
    unnamed x2, local copies, waits for them, and re-layouts  5.29 us

profile of v3, /device:TPU:2, one launch (start us, length us, event | category | flops | bytes accessed | tf_op | source)
XLA Modules:
  0.0 162.9 jit_solution(12958188418806403455)
XLA Ops:
  0.6 157.0 %denoise_attention.1 = (bf16[64,768]{1,0:T(8,128)(2,1)}, bf16[32,64,768]{2,1,0:T(8,128)(2,1)}) custom-call(s32[24]{0:T(128)} %kinds.1, bf16[3,64,768]{2,1,0:T(8,128)(2,1)} %first_hbm.1, bf16[3,32,64,768]{3,2,1,0:T(8,128)(2,1)} %bitcast.3, bf16[96,768]{1,0:T(8,128)(2,1)} %bitcast.5), custom_call_target="tpu_custom_call" | custom-call | tf_op jit(solution)/shard_map/denoise_attention/pallas_call | solution.py:485
  157.6 1.5 copy.8
  159.2 3.8 %copy.9 = bf16[2048,768]{1,0:T(8,128)(2,1)} copy(bf16[2048,768]{1,0:T(8,128)(2,1)} %bitcast.4) | data formatting | bytes 6291456

commit v4 on v3

--- a/solution.py
+++ b/solution.py
@@ -22,6 +22,7 @@
 TW = 2 * HEAD_DIM
 FRAMES = SEQ + 1
 SHARD = 96
+SPLIT = 17
 ROWS = FRAMES * TILE
 HALF_ROWS = FRAMES * HALF
 EXP_SCALE = HEAD_DIM ** (-0.5) * 1.4426950408889634
@@ -333,22 +334,28 @@
         ).start()
         own_t[c, 0] = back[c, 0]
 
-    def ag_copy(c):
+    def pieces(c):
+        return ((0, FRAMES),) if c < CHUNKS - 2 else ((0, SPLIT), (SPLIT, FRAMES - SPLIT))
+
+    def ag_copy(c, i):
+        at = pl.ds(*pieces(c)[i])
         return pltpu.make_async_remote_copy(
-            src_ref=own_t.at[c], dst_ref=near_t.at[c],
-            send_sem=ag_send_sem.at[c], recv_sem=ag_recv_sem.at[c],
+            src_ref=own_t.at[c, at], dst_ref=near_t.at[c, at],
+            send_sem=ag_send_sem.at[c, i], recv_sem=ag_recv_sem.at[c, i],
             device_id=(s, near), device_id_type=MESH,
         )
 
     def share(c):
         landed = own_t.at[c, pl.ds(1, SEQ)]
         pltpu.make_async_copy(landed, landed, back_recv_sem.at[c]).wait()
-        ag_copy(c).start()
-
-    def rs_copy(c):
+        for i in range(len(pieces(c))):
+            ag_copy(c, i).start()
+
+    def rs_copy(c, i):
+        at = pl.ds(*pieces(c)[i])
         return pltpu.make_async_remote_copy(
-            src_ref=part_send.at[c], dst_ref=part_recv.at[c],
-            send_sem=rs_send_sem.at[c], recv_sem=rs_recv_sem.at[c],
+            src_ref=part_send.at[c, at], dst_ref=part_recv.at[c, at],
+            send_sem=rs_send_sem.at[c, i], recv_sem=rs_recv_sem.at[c, i],
             device_id=(s, far), device_id_type=MESH,
         )
 
@@ -361,11 +368,11 @@
             for part, at in ((own, block), (near_half, jnp.bitwise_xor(block, 1)))
         )
 
-    def half_rows(c, spatial_ref, temporal_ref):
+    def half_rows(c, at, spatial_ref, temporal_ref):
         rows = slice((c % 2) * HALF, (c % 2 + 1) * HALF)
-        mixed = temporal_ref[c].astype(f32)
+        mixed = temporal_ref[c, at].astype(f32)
         return jnp.concatenate(
-            [spatial_ref[c // 2].astype(f32)[:, rows], mixed[:, :HALF], mixed[:, HALF:]], axis=2
+            [spatial_ref[c // 2, at].astype(f32)[:, rows], mixed[:, :HALF], mixed[:, HALF:]], axis=2
         )
 
     def pair_rows(c, spatial_ref, temporal_ref):
@@ -382,13 +389,15 @@
                 sp_copy(h).wait_recv()
             first_share.wait_recv()
             w_spread.arrived()
-        ag_copy(c).wait_recv()
-        part = times(half_rows(c, own_s, own_t), half_rows(c, near_s, near_t), far)
-        part = part.reshape(FRAMES, HALF, WIDTH)
-        part_send[c] = jnp.concatenate(
-            [part[:, :, : WIDTH // 2], part[:, :, WIDTH // 2 :]], axis=1
-        ).astype(bf16)
-        rs_copy(c).start()
+        for i, (low, count) in enumerate(pieces(c)):
+            ag_copy(c, i).wait_recv()
+            at = slice(low, low + count)
+            part = times(half_rows(c, at, own_s, own_t), half_rows(c, at, near_s, near_t), far)
+            part = part.reshape(count, HALF, WIDTH)
+            part_send[c, at] = jnp.concatenate(
+                [part[:, :, : WIDTH // 2], part[:, :, WIDTH // 2 :]], axis=1
+            ).astype(bf16)
+            rs_copy(c, i).start()
 
     def own_block(c):
         acc[...] = times(pair_rows(c, own_s, own_t), pair_rows(c, near_s, near_t), g).reshape(
@@ -412,7 +421,8 @@
                 copy.wait()
         halves = []
         for half in range(2):
-            rs_copy(2 * c + half).wait_recv()
+            for i in range(len(pieces(2 * c + half))):
+                rs_copy(2 * c + half, i).wait_recv()
             part = part_recv[2 * c + half].astype(f32)
             halves.append(jnp.concatenate([part[:, :HALF], part[:, HALF:]], axis=2))
         out_buf[c % 2] = (acc[...] + jnp.concatenate(halves, axis=1)).astype(bf16)
@@ -441,21 +451,28 @@
     post_chunk(3)
     first_frame()
     w_spread.third()
-    for step in range(2, CHUNKS):
+    for step in range(2, CHUNKS - 2):
         share(step - 2)
         temporal(step)
-        if step + 2 < CHUNKS:
+        if step + 2 < CHUNKS - 1:
             post_chunk(step + 2)
-        if step == CHUNKS - 1:
-            share(CHUNKS - 2)
         partial(step - 2)
-        if step == CHUNKS - 1:
-            share(CHUNKS - 1)
         if step % 2 == 1:
             own_block((step - 3) // 2)
         elif step >= 4:
             finish((step - 4) // 2)
+    share(CHUNKS - 4)
+    temporal(CHUNKS - 2)
+    post_chunk(CHUNKS - 1)
+    share(CHUNKS - 3)
+    partial(CHUNKS - 4)
+    finish(PAIRS - 3)
+    share(CHUNKS - 2)
+    partial(CHUNKS - 3)
+    own_block(PAIRS - 2)
+    temporal(CHUNKS - 1)
     partial(CHUNKS - 2)
+    share(CHUNKS - 1)
     finish(PAIRS - 2)
     partial(CHUNKS - 1)
     own_block(PAIRS - 1)
@@ -466,8 +483,9 @@
         pltpu.make_async_copy(sent, sent, send_sem.at[c]).wait()
         sent = back.at[c, pl.ds(0, SEQ - 1)]
         pltpu.make_async_copy(sent, sent, back_send_sem.at[c]).wait()
-        ag_copy(c).wait_send()
-        rs_copy(c).wait_send()
+        for i in range(len(pieces(c))):
+            ag_copy(c, i).wait_send()
+            rs_copy(c, i).wait_send()
     for h in range(NS):
         sp_copy(h).wait_send()
     first_share.wait_send()
@@ -476,6 +494,11 @@
     for c in (PAIRS - 2, PAIRS - 1):
         for copy in out_copies(c):
             copy.wait()
+
+
+def hand_over(first, video, first_out, video_out):
+    first_out[...] = first[...]
+    video_out[...] = video[...]
 
 
 def per_device(first_qkv, video_qkv, head_kind, out_weight):
@@ -511,7 +534,7 @@
             pltpu.VMEM((2, FRAMES, TILE, WIDTH), bf16),
             pltpu.VMEM((TILE, ROWS), jnp.float32),
             dma((2,)), dma((2,)), dma((CHUNKS,)), dma((CHUNKS,)), dma((CHUNKS,)), dma((CHUNKS,)),
-            dma((NS + 1,)), dma((NS + 1,)), dma((CHUNKS,)), dma((CHUNKS,)), dma((CHUNKS,)), dma((CHUNKS,)), dma((2, 2)),
+            dma((NS + 1,)), dma((NS + 1,)), dma((CHUNKS, 2)), dma((CHUNKS, 2)), dma((CHUNKS, 2)), dma((CHUNKS, 2)), dma((2, 2)),
             dma((2,)), dma((3,)), dma((3,)), dma((3,)), dma((3,)),
         ],
         compiler_params=pltpu.CompilerParams(
@@ -519,6 +542,23 @@
         ),
         name="denoise_attention",
     )(head_kind, first_qkv, video_qkv.reshape(3, SEQ, 64, WIDTH), out_weight.T)
+    first_out, video_out = pl.pallas_call(
+        hand_over,
+        out_shape=(
+            jax.ShapeDtypeStruct((64, WIDTH), bf16),
+            jax.ShapeDtypeStruct((SEQ, 64, WIDTH), bf16),
+        ),
+        grid=(4,),
+        in_specs=[
+            pl.BlockSpec((16, WIDTH), lambda i: (i, 0)),
+            pl.BlockSpec((SEQ // 4, 64, WIDTH), lambda i: (i, 0, 0)),
+        ],
+        out_specs=(
+            pl.BlockSpec((16, WIDTH), lambda i: (i, 0)),
+            pl.BlockSpec((SEQ // 4, 64, WIDTH), lambda i: (i, 0, 0)),
+        ),
+        name="hand_over",
+    )(first_out, video_out)
     return first_out, video_out.reshape(F, WIDTH)
 
 

time: 165 us -> 162 us (0.982)
  local copies, waits for them, and re-layouts: 5.29 us -> 0 us
  Pallas kernels: 157 us -> 160 us
    unnamed x2 -> x0, local copies, waits for them, and re-layouts: 5.29 us -> none
    pallas_call x0 -> x1, Pallas kernels: none -> 4.25 us  [per_device(): pl.pallas_call(hand_over, out_shape=(jax.ShapeDtypeStruct((64, WIDTH), bf...]
where the time goes in v4:
time: 162 us; the launch traced here: 161 us
  Pallas kernels  160 us (99%)
    pallas_call x1, Pallas kernels, per_device(): pl.pallas_call(kernel, out_shape=(jax.ShapeDtypeStruct((64, WIDTH), bf16)...  156 us
    pallas_call x1, Pallas kernels, per_device(): pl.pallas_call(hand_over, out_shape=(jax.ShapeDtypeStruct((64, WIDTH), bf...  4.25 us

profile of v4, /device:TPU:2, one launch (start us, length us, event | category | flops | bytes accessed | tf_op | source)
XLA Modules:
  0.0 160.7 jit_solution(17331512033188844121)
XLA Ops:
  0.6 155.8 %denoise_attention.1 = (bf16[64,768]{1,0:T(8,128)(2,1)}, bf16[32,64,768]{2,1,0:T(8,128)(2,1)}) custom-call(s32[24]{0:T(128)} %kinds.1, bf16[3,64,768]{2,1,0:T(8,128)(2,1)} %first_hbm.1, bf16[3,32,64,768]{3,2,1,0:T(8,128)(2,1)} %bitcast.3, bf16[96,768]{1,0:T(8,128)(2,1)} %bitcast.4), custom_call_target="tpu_custom_call" | custom-call | tf_op jit(solution)/shard_map/denoise_attention/pallas_call | solution.py:508
  156.5 4.2 %hand_over.1 = (bf16[64,768]{1,0:T(8,128)(2,1)}, bf16[32,64,768]{2,1,0:T(8,128)(2,1)}) custom-call(bf16[64,768]{1,0:T(8,128)(2,1)} %get-tuple-element.6.first, bf16[32,64,768]{2,1,0:T(8,128)(2,1)} %get-tuple-element.7.video), custom_call_target="tpu_custom_call" | custom-call | tf_op jit(solution)/shard_map/hand_over/pallas_call | solution.py:545

commit v5 on v4

--- a/solution.py
+++ b/solution.py
@@ -160,21 +160,28 @@
             device_id=(target, g), device_id_type=MESH,
         ).start()
 
+    def on_z(k):
+        return y * 8 + ((z + k) % 4) * 2 + core
+
+    def on_y(k):
+        return ((y + k) % 4) * 8 + z * 2 + core
+
     def along_z(ref, sems):
         for k in range(1, 4):
-            to_seq(ref, y * 8 + ((z + k) % 4) * 2 + core, sems)
+            to_seq(ref, on_z(k), sems)
 
     def along_y(ref, sems):
         for k in range(1, 4):
-            to_seq(ref, ((y + k) % 4) * 8 + z * 2 + core, sems)
+            to_seq(ref, on_y(k), sems)
 
     def await_bytes(ref, sem):
         pltpu.make_async_copy(ref, ref, sem).wait()
 
     class Spread:
-        def __init__(self, buf, send_sems, recv_sems):
+        def __init__(self, buf, halves, send_sems, recv_sems):
             self.buf = buf
-            self.sems = [(send_sems.at[i], recv_sems.at[i]) for i in range(3)]
+            self.halves = halves
+            self.sems = [(send_sems.at[i], recv_sems.at[i]) for i in range(4)]
 
         def first(self):
             @pl.when(core == 0)
@@ -190,14 +197,29 @@
 
             @pl.when(core == 0)
             def _():
-                along_y(self.buf.at[y, :, core], self.sems[1])
+                for k in (1, 3):
+                    to_seq(self.buf.at[y, :, core], on_y(k), self.sems[1])
 
             @pl.when(core == 1)
             def _():
-                along_z(self.buf.at[:, z, core], self.sems[1])
+                for k in (1, 3):
+                    to_seq(self.buf.at[:, z, core], on_z(k), self.sems[1])
+
+        def relay(self):
+            await_bytes(self.buf.at[pl.ds(0, 2), :, core], self.sems[1][1])
+
+            @pl.when(core == 0)
+            def _():
+                for k, half in ((1, self.halves[0]), (3, self.halves[1])):
+                    to_seq(self.buf.at[(y + 4 - k) % 4, :, core, *half], on_y(k), self.sems[3])
+
+            @pl.when(core == 1)
+            def _():
+                for k, half in ((1, self.halves[0]), (3, self.halves[1])):
+                    to_seq(self.buf.at[:, (z + 4 - k) % 4, core, *half], on_z(k), self.sems[3])
 
         def third(self):
-            await_bytes(self.buf.at[pl.ds(0, 3), :, core], self.sems[1][1])
+            await_bytes(self.buf.at[0, :, core], self.sems[3][1])
             to_seq(self.buf.at[:, :, core], s + 1 - 2 * core, self.sems[2])
 
         def arrived(self):
@@ -205,11 +227,16 @@
 
         def sent(self):
             await_bytes(self.buf.at[0, pl.ds(0, 3), core], self.sems[0][0])
-            await_bytes(self.buf.at[pl.ds(0, 3), :, core], self.sems[1][0])
+            await_bytes(self.buf.at[pl.ds(0, 2), :, core], self.sems[1][0])
+            await_bytes(self.buf.at[0, :, core], self.sems[3][0])
             await_bytes(self.buf.at[:, :, core], self.sems[2][0])
 
-    kv_spread = Spread(kv, kv_send_sem, kv_recv_sem)
-    w_spread = Spread(weight, w_send_sem, w_recv_sem)
+    kv_spread = Spread(
+        kv, [(slice(None), pl.ds(i * 32, 32)) for i in range(2)], kv_send_sem, kv_recv_sem
+    )
+    w_spread = Spread(
+        weight, [(pl.ds(i * 48, 48),) for i in range(2)], w_send_sem, w_recv_sem
+    )
 
 
     def pack_chunk(c):
@@ -443,10 +470,12 @@
     pack_chunk(3)
     w_spread.second()
     frame_head(0)
+    kv_spread.relay()
     temporal(0)
     post_chunk(2)
+    frame_head(1)
+    w_spread.relay()
     kv_spread.third()
-    frame_head(1)
     temporal(1)
     post_chunk(3)
     first_frame()
@@ -535,7 +564,7 @@
             pltpu.VMEM((TILE, ROWS), jnp.float32),
             dma((2,)), dma((2,)), dma((CHUNKS,)), dma((CHUNKS,)), dma((CHUNKS,)), dma((CHUNKS,)),
             dma((NS + 1,)), dma((NS + 1,)), dma((CHUNKS, 2)), dma((CHUNKS, 2)), dma((CHUNKS, 2)), dma((CHUNKS, 2)), dma((2, 2)),
-            dma((2,)), dma((3,)), dma((3,)), dma((3,)), dma((3,)),
+            dma((2,)), dma((4,)), dma((4,)), dma((4,)), dma((4,)),
         ],
         compiler_params=pltpu.CompilerParams(
             collective_id=0, has_side_effects=True, vmem_limit_bytes=62 * 2**20

time: 162 us -> 157 us (0.969)
  Pallas kernels: 160 us -> 155 us
    pallas_call x1, Pallas kernels: 156 us -> 151 us  [per_device(): pl.pallas_call(kernel, out_shape=(jax.ShapeDtypeStruct((64, WIDTH), bf16)...]
where the time goes in v5:
time: 157 us; the launch traced here: 156 us
  Pallas kernels  155 us (99%)
    pallas_call x1, Pallas kernels, per_device(): pl.pallas_call(kernel, out_shape=(jax.ShapeDtypeStruct((64, WIDTH), bf16)...  151 us
    pallas_call x1, Pallas kernels, per_device(): pl.pallas_call(hand_over, out_shape=(jax.ShapeDtypeStruct((64, WIDTH), bf...  4.25 us

profile of v5, /device:TPU:2, one launch (start us, length us, event | category | flops | bytes accessed | tf_op | source)
XLA Modules:
  0.0 156.0 jit_solution(12119672635431639364)
XLA Ops:
  0.6 151.2 %denoise_attention.1 = (bf16[64,768]{1,0:T(8,128)(2,1)}, bf16[32,64,768]{2,1,0:T(8,128)(2,1)}) custom-call(s32[24]{0:T(128)} %kinds.1, bf16[3,64,768]{2,1,0:T(8,128)(2,1)} %first_hbm.1, bf16[3,32,64,768]{3,2,1,0:T(8,128)(2,1)} %bitcast.3, bf16[96,768]{1,0:T(8,128)(2,1)} %bitcast.4), custom_call_target="tpu_custom_call" | custom-call | tf_op jit(solution)/shard_map/denoise_attention/pallas_call | solution.py:537
  151.8 4.2 %hand_over.1 = (bf16[64,768]{1,0:T(8,128)(2,1)}, bf16[32,64,768]{2,1,0:T(8,128)(2,1)}) custom-call(bf16[64,768]{1,0:T(8,128)(2,1)} %get-tuple-element.6.first, bf16[32,64,768]{2,1,0:T(8,128)(2,1)} %get-tuple-element.7.video), custom_call_target="tpu_custom_call" | custom-call | tf_op jit(solution)/shard_map/hand_over/pallas_call | solution.py:574
